TPU v7x, 32 devices: a whole 2x2x4 slice. The times are simulated.
32 devices in a mesh: rep: 8 (over z, y), shard: 4 (over x, core).
Axes of the slice: x: 2, y: 2, z: 4, core: 2. Of those that a mesh axis runs over, the one named last changes fastest.
Arguments:
- hidden_in: bfloat16 [4096, 960], P(('rep', 'shard')), may hold values from -6 to 6
- segment_ids: int32 [4096], P(('rep', 'shard')), may hold values from 0 to 31, as said below
- positions: int32 [4096], P(('rep', 'shard')), may hold values from 0 to 511, as said below
- norm_attn: bfloat16 [960], P('shard'), may hold values from 0.5 to 1.5
- w_query: bfloat16 [960, 960], P('shard'), may hold values from -0.19364917 to 0.19364917
- w_key: bfloat16 [960, 320], P('shard'), may hold values from -0.19364917 to 0.19364917
- w_value: bfloat16 [960, 320], P('shard'), may hold values from -0.1875 to 0.1875
- w_out: bfloat16 [960, 960], P('shard'), may hold values from -1.5 to 1.5
- norm_mlp: bfloat16 [960], P('shard'), may hold values from 0.29882812 to 3
- w_gate: bfloat16 [960, 2560], P('shard'), may hold values from -0.1875 to 0.1875
- w_up: bfloat16 [960, 2560], P('shard'), may hold values from -0.1875 to 0.1875
- w_down: bfloat16 [2560, 960], P('shard'), may hold values from -0.25 to 0.25
- grad_out: bfloat16 [4096, 960], P(('rep', 'shard')), may hold values from -6 to 6
Outputs:
- output: bfloat16 [4096, 960], P(('rep', 'shard'))
- grad_hidden: float32 [4096, 960], P(('rep', 'shard'))
- grad_norm_attn: float32 [960], P('shard')
- grad_w_query: float32 [960, 960], P('shard')
- grad_w_key: float32 [960, 320], P('shard')
- grad_w_value: float32 [960, 320], P('shard')
- grad_w_out: float32 [960, 960], P('shard')
- grad_norm_mlp: float32 [960], P('shard')
- grad_w_gate: float32 [960, 2560], P('shard')
- grad_w_up: float32 [960, 2560], P('shard')
- grad_w_down: float32 [2560, 960], P('shard')
Inputs may be any that keep to these rules, and one draw needn't show every extreme that they name: `segment_ids`: within each row of 512 consecutive tokens the ids never fall, and no two rows share an id. Within a segment positions rise by one from token to token; the first segment of a row may begin above 0, every other begins at 0.
All inputs are finite; a program needn't handle non-finite values.
Results may differ from a plain program's by a relative error of at most 0.019.
Values may be sent and summed in bfloat16 or wider, within the bound.
A program may use at most 192 MiB of HBM per device.

v0:
```python
import math

import jax
import jax.numpy as jnp
from jax import lax
from jax.sharding import PartitionSpec as P

H = 15
KV = 5
HD = 64


EPS = 1e-05
THETA = 100000.0
NEG = -1e30


def rope_tables(positions, head_size):
    half_size = head_size // 2
    frequency = THETA ** (-(jnp.arange(half_size, dtype=jnp.float32) * 2.0 / head_size))
    angles = positions.astype(jnp.float32)[:, None] * frequency[None, :]
    return (jnp.cos(angles), jnp.sin(angles))


def rotate(values, cosine, sine, direction):
    half_size = values.shape[-1] // 2
    first_half = values[..., :half_size]
    second_half = values[..., half_size:]
    cos_table = cosine[:, None, :]
    sin_table = sine[:, None, :] * direction
    return jnp.concatenate(
        [
            first_half * cos_table - second_half * sin_table,
            second_half * cos_table + first_half * sin_table,
        ],
        axis=-1,
    )


def norm_forward(values, gain):
    inverse = lax.rsqrt(jnp.mean(values * values, axis=-1, keepdims=True) + EPS)
    return (values * inverse * gain, inverse)


def norm_backward(values, inverse, gain, upstream):
    scaled = upstream * gain
    grad_gain = jnp.sum(upstream * values * inverse, axis=0)
    inner = jnp.mean(scaled * values, axis=-1, keepdims=True)
    return (inverse * scaled - values * inverse * inverse * inverse * inner, grad_gain)


def allowed_mask(query_seg, query_idx, key_seg, key_idx):
    return (query_seg[:, None] == key_seg[None, :]) & (key_idx[None, :] <= query_idx[:, None])


def left_product(left, right):
    return jnp.dot(left.T, right, preferred_element_type=jnp.float32)


def local(
    hidden_in,
    segment_ids,
    positions,
    norm_attn,
    w_query,
    w_key,
    w_value,
    w_out,
    norm_mlp,
    w_gate,
    w_up,
    w_down,
    grad_out,
):
    tok_rows = hidden_in.shape[0]
    row_len = tok_rows * lax.axis_size("shard")
    first_row = lax.axis_index("shard") * tok_rows
    last_row = first_row + tok_rows - 1
    groups = H // KV
    score_scale = 1.0 / math.sqrt(HD)
    query_idx = first_row + jnp.arange(tok_rows, dtype=jnp.int32)
    row_segments = lax.all_gather(segment_ids, "shard", axis=0, tiled=True)
    attn_full = (
        lax.all_gather(norm_attn, "shard", axis=0, tiled=True),
        lax.all_gather(w_query, "shard", axis=0, tiled=True),
        lax.all_gather(w_key, "shard", axis=0, tiled=True),
        lax.all_gather(w_value, "shard", axis=0, tiled=True),
        lax.all_gather(w_out, "shard", axis=0, tiled=True),
    )
    mlp_full = (
        lax.all_gather(norm_mlp, "shard", axis=0, tiled=True),
        lax.all_gather(w_gate, "shard", axis=0, tiled=True),
        lax.all_gather(w_up, "shard", axis=0, tiled=True),
        lax.all_gather(w_down, "shard", axis=0, tiled=True),
    )

    def key_mask(count):
        key_idx = jnp.arange(count, dtype=jnp.int32)
        return allowed_mask(segment_ids, query_idx, row_segments, key_idx)[:, None, None, :]

    resid = hidden_in.astype(jnp.float32)
    normed, inv_attn = norm_forward(resid, attn_full[0].astype(jnp.float32))
    normed_b = normed.astype(jnp.bfloat16)
    cos_table, sin_table = rope_tables(positions, HD)
    query = jnp.dot(normed_b, attn_full[1], preferred_element_type=jnp.float32).reshape(
        tok_rows, H, HD
    )
    query_b = rotate(query, cos_table, sin_table, 1.0).astype(jnp.bfloat16)
    keys = jnp.dot(normed_b, attn_full[2], preferred_element_type=jnp.float32).reshape(
        tok_rows, KV, HD
    )
    key_b = rotate(keys, cos_table, sin_table, 1.0).astype(jnp.bfloat16)
    value_b = (
        jnp.dot(normed_b, attn_full[3], preferred_element_type=jnp.float32)
        .astype(jnp.bfloat16)
        .reshape(tok_rows, KV, HD)
    )
    query4 = query_b.reshape(tok_rows, KV, groups, HD)
    start_state = (
        jnp.full((tok_rows, KV, groups), NEG, jnp.float32),
        jnp.zeros((tok_rows, KV, groups), jnp.float32),
        jnp.zeros((tok_rows, KV, groups, HD), jnp.float32),
    )
    key_piece = lax.all_gather(key_b, "shard", axis=0, tiled=True)
    value_piece = lax.all_gather(value_b, "shard", axis=0, tiled=True)
    count = key_piece.shape[0]

    def forward_attend(inner):
        row_max, row_sum, accum = inner
        allowed = key_mask(count)
        scores = (
            jnp.einsum("tgrd,jgd->tgrj", query4, key_piece, preferred_element_type=jnp.float32)
            * score_scale
        )
        scores = jnp.where(allowed, scores, NEG)
        new_max = jnp.maximum(row_max, jnp.max(scores, axis=-1))
        weights = jnp.where(allowed, jnp.exp(scores - new_max[..., None]), 0.0)
        row_sum = jnp.sum(weights, axis=-1)
        accum = jnp.einsum("tgrj,jgd->tgrd", weights, value_piece.astype(jnp.float32))
        return (new_max, row_sum, accum)

    row_max, row_sum, accum = lax.cond(
        jnp.int32(0) > last_row, lambda inner: inner, forward_attend, start_state
    )
    attn4 = (accum / row_sum[..., None]).astype(jnp.bfloat16)
    attn_b = attn4.reshape(tok_rows, H * HD)
    log_total = row_max + jnp.log(row_sum)
    mixed = resid + jnp.dot(attn_b, attn_full[4], preferred_element_type=jnp.float32)
    normed_mlp, inv_mlp = norm_forward(mixed, mlp_full[0].astype(jnp.float32))
    normed_mlp_b = normed_mlp.astype(jnp.bfloat16)
    gate = jnp.dot(normed_mlp_b, mlp_full[1], preferred_element_type=jnp.float32)
    upper = jnp.dot(normed_mlp_b, mlp_full[2], preferred_element_type=jnp.float32)
    sigma = jax.nn.sigmoid(gate)
    act_b = (gate * sigma * upper).astype(jnp.bfloat16)
    result = (mixed + jnp.dot(act_b, mlp_full[3], preferred_element_type=jnp.float32)).astype(
        jnp.bfloat16
    )
    mlp_back = (
        lax.all_gather(norm_mlp, "shard", axis=0, tiled=True),
        lax.all_gather(w_gate, "shard", axis=0, tiled=True),
        lax.all_gather(w_up, "shard", axis=0, tiled=True),
        lax.all_gather(w_down, "shard", axis=0, tiled=True),
    )
    attn_back = (
        lax.all_gather(norm_attn, "shard", axis=0, tiled=True),
        lax.all_gather(w_query, "shard", axis=0, tiled=True),
        lax.all_gather(w_key, "shard", axis=0, tiled=True),
        lax.all_gather(w_value, "shard", axis=0, tiled=True),
        lax.all_gather(w_out, "shard", axis=0, tiled=True),
    )
    grad_act = jnp.dot(grad_out, mlp_back[3].T, preferred_element_type=jnp.float32)
    grad_gate_b = (grad_act * upper * sigma * (1.0 + gate * (1.0 - sigma))).astype(jnp.bfloat16)
    grad_up_b = (grad_act * gate * sigma).astype(jnp.bfloat16)
    grad_normed_mlp = jnp.dot(
        grad_gate_b, mlp_back[1].T, preferred_element_type=jnp.float32
    ) + jnp.dot(grad_up_b, mlp_back[2].T, preferred_element_type=jnp.float32)
    grad_mixed_n, grad_gain_mlp = norm_backward(
        mixed, inv_mlp, mlp_back[0].astype(jnp.float32), grad_normed_mlp
    )
    grad_mixed = grad_out.astype(jnp.float32) + grad_mixed_n
    grad_mixed_b = grad_mixed.astype(jnp.bfloat16)
    grad_attn_b = jnp.dot(grad_mixed_b, attn_back[4].T, preferred_element_type=jnp.float32).astype(
        jnp.bfloat16
    )
    grad_attn4 = grad_attn_b.reshape(tok_rows, KV, groups, HD)
    delta = jnp.sum(grad_attn4.astype(jnp.float32) * attn4.astype(jnp.float32), axis=-1)
    back_state = (
        jnp.zeros((tok_rows, KV, groups, HD), jnp.float32),
        jnp.zeros((row_len, KV, HD), jnp.float32),
        jnp.zeros((row_len, KV, HD), jnp.float32),
    )
    backward_key_piece = lax.all_gather(key_b, "shard", axis=0, tiled=True)
    backward_value_piece = lax.all_gather(value_b, "shard", axis=0, tiled=True)
    backward_count = backward_key_piece.shape[0]

    def backward_attend(inner):
        allowed = key_mask(backward_count)
        scores = (
            jnp.einsum(
                "tgrd,jgd->tgrj", query4, backward_key_piece, preferred_element_type=jnp.float32
            )
            * score_scale
        )
        scores = jnp.where(allowed, scores, NEG)
        probs = jnp.where(allowed, jnp.exp(scores - log_total[..., None]), 0.0)
        value_part = jnp.einsum(
            "tgrj,tgrd->jgd",
            probs.astype(jnp.bfloat16),
            grad_attn4,
            preferred_element_type=jnp.float32,
        )
        grad_probs = jnp.einsum(
            "tgrd,jgd->tgrj", grad_attn4, backward_value_piece, preferred_element_type=jnp.float32
        )
        grad_scores = (probs * (grad_probs - delta[..., None])).astype(jnp.bfloat16)
        grad_query = (
            jnp.einsum(
                "tgrj,jgd->tgrd",
                grad_scores,
                backward_key_piece,
                preferred_element_type=jnp.float32,
            )
            * score_scale
        )
        key_part = (
            jnp.einsum("tgrj,tgrd->jgd", grad_scores, query4, preferred_element_type=jnp.float32)
            * score_scale
        )
        return (grad_query, key_part, value_part)

    grad_query, grad_keys, grad_values = lax.cond(
        jnp.int32(0) > last_row, lambda inner: inner, backward_attend, back_state
    )
    own_keys, own_values = (
        lax.psum_scatter(grad_keys, "shard", scatter_dimension=0, tiled=True),
        lax.psum_scatter(grad_values, "shard", scatter_dimension=0, tiled=True),
    )
    grad_query_b = (
        rotate(grad_query.reshape(tok_rows, H, HD), cos_table, sin_table, -1.0)
        .astype(jnp.bfloat16)
        .reshape(tok_rows, H * HD)
    )
    grad_key_b = (
        rotate(own_keys, cos_table, sin_table, -1.0).astype(jnp.bfloat16).reshape(tok_rows, KV * HD)
    )
    grad_value_b = own_values.astype(jnp.bfloat16).reshape(tok_rows, KV * HD)
    grad_normed = jnp.dot(grad_query_b, attn_back[1].T, preferred_element_type=jnp.float32)
    grad_normed = grad_normed + jnp.dot(
        grad_key_b, attn_back[2].T, preferred_element_type=jnp.float32
    )
    grad_normed = grad_normed + jnp.dot(
        grad_value_b, attn_back[3].T, preferred_element_type=jnp.float32
    )
    grad_resid_n, grad_gain_attn = norm_backward(
        resid, inv_attn, attn_back[0].astype(jnp.float32), grad_normed
    )
    grad_hidden = grad_mixed + grad_resid_n
    grad_w_down = left_product(act_b, grad_out)
    grad_w_gate = left_product(normed_mlp_b, grad_gate_b)
    grad_w_up = left_product(normed_mlp_b, grad_up_b)
    grad_w_out = left_product(attn_b, grad_mixed_b)
    grad_w_query = left_product(normed_b, grad_query_b)
    grad_w_key = left_product(normed_b, grad_key_b)
    grad_w_value = left_product(normed_b, grad_value_b)
    totals = lax.psum(
        (
            lax.psum_scatter(grad_gain_attn, "shard", scatter_dimension=0, tiled=True),
            lax.psum_scatter(grad_w_query, "shard", scatter_dimension=0, tiled=True),
            lax.psum_scatter(grad_w_key, "shard", scatter_dimension=0, tiled=True),
            lax.psum_scatter(grad_w_value, "shard", scatter_dimension=0, tiled=True),
            lax.psum_scatter(grad_w_out, "shard", scatter_dimension=0, tiled=True),
            lax.psum_scatter(grad_gain_mlp, "shard", scatter_dimension=0, tiled=True),
            lax.psum_scatter(grad_w_gate, "shard", scatter_dimension=0, tiled=True),
            lax.psum_scatter(grad_w_up, "shard", scatter_dimension=0, tiled=True),
            lax.psum_scatter(grad_w_down, "shard", scatter_dimension=0, tiled=True),
        ),
        "rep",
    )
    return (
        result,
        grad_hidden,
        totals[0],
        totals[1],
        totals[2],
        totals[3],
        totals[4],
        totals[5],
        totals[6],
        totals[7],
        totals[8],
    )


def solution(mesh):
    placed = (
        P(("rep", "shard"), None),
        P(("rep", "shard")),
        P(("rep", "shard")),
        P("shard"),
        P("shard", None),
        P("shard", None),
        P("shard", None),
        P("shard", None),
        P("shard"),
        P("shard", None),
        P("shard", None),
        P("shard", None),
        P(("rep", "shard"), None),
    )
    return jax.shard_map(
        local,
        mesh=mesh,
        in_specs=placed,
        out_specs=(
            P(("rep", "shard"), None),
            P(("rep", "shard"), None),
            P("shard"),
            P("shard", None),
            P("shard", None),
            P("shard", None),
            P("shard", None),
            P("shard"),
            P("shard", None),
            P("shard", None),
            P("shard", None),
        ),
        check_vma=False,
    )
```

profile of v0, /device:TPU:0, one launch (start us, length us, event | category | flops | bytes accessed | tf_op | source)
XLA Modules:
  0.0 1004.5 jit_solution(6734099215301849498)
XLA Ops:
  12.5 8.3 all-reduce.7
  20.8 11.4 %all-gather.1 = bf16[4,240,320]{1,2,0:T(8,128)(2,1)S(1)} all-gather(bf16[1,240,320]{1,2,0:T(8,128)(2,1)S(1)} %bitcast.153), channel_id=1, replica_groups=mesh['rep'=8,'shard'=4] {'shard'}, dimensions={0}, use_global_device_ids=true | all-gather | bytes 768000 | tf_op jit(solution)/shard_map/all_gather | solution.py:86
  33.3 8.0 all-gather.2
  42.4 5.0 all-gather
  48.2 8.3 all_gather.50
  57.0 7.5 all_gather.53
  67.2 3.9 conditional.2
  75.0 28.3 %all-gather.15.cloned.1.call-done = bf16[960,2560]{1,0:T(8,128)(2,1)} async-done(((bf16[240,2560]{1,0:T(8,128)(2,1)}), bf16[960,2560]{1,0:T(8,128)(2,1)}) %all-gather.15.cloned.1.call-update) | async-done | bytes 4915216 | tf_op jit(solution)/shard_map/all_gather | solution.py:93
  103.3 4.3 fusion.70
  107.6 35.7 %all-gather.13.cloned.1.call-done = bf16[960,2560]{1,0:T(8,128)(2,1)} async-done(((bf16[240,2560]{1,0:T(8,128)(2,1)}), bf16[960,2560]{1,0:T(8,128)(2,1)}) %all-gather.13.cloned.1.call-update) | async-done | bytes 4915216 | tf_op jit(solution)/shard_map/all_gather | solution.py:92
  143.3 4.3 fusion.69
  147.7 35.7 %all-gather.17.cloned.1.call-done = bf16[2560,960]{0,1:T(8,128)(2,1)} async-done(((bf16[640,960]{0,1:T(8,128)(2,1)}), bf16[2560,960]{0,1:T(8,128)(2,1)}) %all-gather.17.cloned.1.call-update) | async-done | bytes 4915216 | tf_op jit(solution)/shard_map/all_gather | solution.py:94
  183.3 5.5 multiply_convert_fusion
  190.3 4.1 multiply_reduce_fusion
  195.4 13.9 %conditional.3 = (f32[512,5,64]{0,2,1:T(8,128)S(1)}, f32[512,5,64]{0,2,1:T(8,128)}, f32[128,15,32]{0,2,1:T(8,128)S(1)}, f32[128,15,32]{0,2,1:T(8,128)S(1)}) conditional(s32[]{:T(128)} %convert_element_type.83, (s32[128]{0:T(128)S(1)}, s32[512]{0:T(512)S(1)}, s32[128]{0:T(128)S(1)}, bf16[512,5,64]{0,2,1:T(8,128)(2,1)S(1)}, ...), branch_computations={%region_8.9_spmd, %region_9.10_spmd} | conditional | flops 641794048 | bytes 26892892 | solution.py:231
  198.7 2.9 fusion.25
  210.2 21.7 %reduce-scatter.16.cloned.1.call-done = f32[128,5,64]{0,2,1:T(8,128)} async-done(((f32[512,5,64]{0,2,1:T(8,128)}), f32[128,5,64]{0,2,1:T(8,128)}) %reduce-scatter.16.cloned.1.call-update) | async-done | bytes 163856 | tf_op jit(solution)/shard_map/reduce_scatter | solution.py:236
  234.5 23.0 %reduce-scatter.14.cloned.1.call-done = f32[128,5,64]{0,2,1:T(8,128)} async-done(((f32[512,5,64]{0,2,1:T(8,128)}), f32[128,5,64]{0,2,1:T(8,128)}) %reduce-scatter.14.cloned.1.call-update) | async-done | bytes 163856 | tf_op jit(solution)/shard_map/reduce_scatter | solution.py:235
  266.3 5.2 fusion.76
  272.6 5.2 fusion.75
  278.9 5.1 fusion.74
  284.3 3.9 reduce-scatter.30.cloned.1.call-done
  290.1 29.1 %reduce-scatter.28.cloned.1.call-done = f32[240,320]{1,0:T(8,128)} async-done(((f32[960,320]{1,0:T(8,128)}), f32[240,320]{1,0:T(8,128)}) %reduce-scatter.28.cloned.1.call-update) | async-done | bytes 307216
  321.0 43.4 %reduce-scatter.20.cloned.1.call-done = f32[240,960]{1,0:T(8,128)} async-done(((f32[960,960]{1,0:T(8,128)}), f32[240,960]{1,0:T(8,128)}) %reduce-scatter.20.cloned.1.call-update) | async-done | bytes 921616 | tf_op jit(solution)/shard_map/reduce_scatter | solution.py:271
  364.5 45.6 %reduce-scatter.18.cloned.1.call-done = f32[240,960]{1,0:T(8,128)} async-done(((f32[960,960]{1,0:T(8,128)}), f32[240,960]{1,0:T(8,128)}) %reduce-scatter.18.cloned.1.call-update) | async-done | bytes 921616 | tf_op jit(solution)/shard_map/reduce_scatter | solution.py:268
  410.1 83.5 %reduce-scatter.26.cloned.1.call-done = f32[640,960]{0,1:T(8,128)} async-done(((f32[2560,960]{0,1:T(8,128)}), f32[640,960]{0,1:T(8,128)}) %reduce-scatter.26.cloned.1.call-update) | async-done | bytes 2457616 | tf_op jit(solution)/shard_map/reduce_scatter | solution.py:275
  493.6 83.7 %reduce-scatter.24.cloned.1.call-done = f32[240,2560]{1,0:T(8,128)} async-done(((f32[960,2560]{1,0:T(8,128)}), f32[240,2560]{1,0:T(8,128)}) %reduce-scatter.24.cloned.1.call-update) | async-done | bytes 2457616 | tf_op jit(solution)/shard_map/reduce_scatter | solution.py:274
  577.3 83.5 %reduce-scatter.22.cloned.1.call-done = f32[240,2560]{1,0:T(8,128)} async-done(((f32[960,2560]{1,0:T(8,128)}), f32[240,2560]{1,0:T(8,128)}) %reduce-scatter.22.cloned.1.call-update) | async-done | bytes 2457616 | tf_op jit(solution)/shard_map/reduce_scatter | solution.py:273
  661.6 4.7 fusion.40
  668.0 5.9 all-reduce.6
  674.0 23.0 %all-reduce.4 = (f32[240]{0:T(256)}, f32[240]{0:T(256)}) all-reduce(f32[240]{0:T(256)S(1)} %dynamic-slice.3, f32[240]{0:T(256)S(1)} %dynamic-slice.5), channel_id=1, replica_groups=mesh['rep'=8,'shard'=4] {'rep'}, use_global_device_ids=true, to_apply=%region_15.16 | all-reduce | flops 480 | bytes 3840 | tf_op jit(solution)/shard_map/psum | solution.py:265
  698.1 287.2 %all-reduce.10.cloned.1.call-done = (f32[240,960]{1,0:T(8,128)}, f32[240,320]{0,1:T(8,128)}, f32[240,320]{0,1:T(8,128)}, f32[240,960]{1,0:T(8,128)}, f32[240,256...) async-done(((f32[240,960]{1,0:T(8,128)}, f32[240,320]{0,1:T(8,128)}, f32[240,320]{0,1:T(8,128)}, f32[240,960]{1,0:T(8,128)}, f32[240,2560]{1,0:T(8,128)}, ...) | async-done | bytes 9830416 | tf_op jit(solution)/shard_map/psum | solution.py:265
  (176 shorter events, 65.3 us)
Async XLA Ops:
  7.2 13.6 %copy-start.28 = (bf16[240,320]{0,1:T(8,128)(2,1)S(1)}, bf16[240,320]{0,1:T(8,128)(2,1)}, u32[]{:S(2)}) copy-start(bf16[240,320]{0,1:T(8,128)(2,1)} %param.22) | copy-start | bytes 460804
  7.2 57.2 %all-gather.9.cloned.1.call-start = ((), (), s32[]{:S(2)}) async-start(), calls=%async_computation.9 | async-start | bytes 2457600 | tf_op jit(solution)/shard_map/all_gather | solution.py:85
  8.0 25.3 %copy-start.29 = (bf16[240,320]{0,1:T(8,128)(2,1)S(1)}, bf16[240,320]{0,1:T(8,128)(2,1)}, u32[]{:S(2)}) copy-start(bf16[240,320]{0,1:T(8,128)(2,1)} %param.23) | copy-start | bytes 460804
  8.0 64.1 %all-gather.11.cloned.1.call-start = ((), (), s32[]{:S(2)}) async-start(), calls=%async_computation.10 | async-start | bytes 2457600 | tf_op jit(solution)/shard_map/all_gather | solution.py:88
  8.7 94.6 %all-gather.15.cloned.1.call-start = ((), (), s32[]{:S(2)}) async-start(), calls=%async_computation.12 | async-start | bytes 6144000 | tf_op jit(solution)/shard_map/all_gather | solution.py:93
  9.5 133.9 %all-gather.13.cloned.1.call-start = ((), (), s32[]{:S(2)}) async-start(), calls=%async_computation.11 | async-start | bytes 6144000 | tf_op jit(solution)/shard_map/all_gather | solution.py:92
  10.0 32.3 %copy-start.30 = (s32[128]{0:T(128)S(1)}, s32[128]{0:T(128)}, u32[]{:S(2)}) copy-start(s32[128]{0:T(128)} %param.18) | copy-start | bytes 1540
  10.0 37.4 %copy-start.1 = (bf16[128,960]{0,1:T(8,128)(2,1)S(1)}, bf16[128,960]{0,1:T(8,128)(2,1)}, u32[]{:S(2)}) copy-start(bf16[128,960]{0,1:T(8,128)(2,1)} %param.17) | copy-start | bytes 737284
  10.1 173.3 %all-gather.17.cloned.1.call-start = ((), (), s32[]{:S(2)}) async-start(), calls=%async_computation.13 | async-start | bytes 6144000 | tf_op jit(solution)/shard_map/all_gather | solution.py:94
  10.6 221.3 %reduce-scatter.16.cloned.1.call-start = ((), (), s32[]{:S(2)}) async-start(), calls=%async_computation.15 | async-start | bytes 819200 | tf_op jit(solution)/shard_map/reduce_scatter | solution.py:236
  33.3 33.8 %copy-start.9 = (bf16[960,320]{0,1:T(8,128)(2,1)}, bf16[960,320]{0,1:T(8,128)(2,1)S(1)}, u32[]{:S(2)}) copy-start(bf16[960,320]{0,1:T(8,128)(2,1)S(1)} %reshape.260) | copy-start | bytes 1843204
  42.3 24.9 %copy-start.11 = (bf16[960,320]{0,1:T(8,128)(2,1)}, bf16[960,320]{0,1:T(8,128)(2,1)S(1)}, u32[]{:S(2)}) copy-start(bf16[960,320]{0,1:T(8,128)(2,1)S(1)} %reshape.262) | copy-start | bytes 1843204
  107.6 75.7 %copy-start.21 = (bf16[128,960]{0,1:T(8,128)(2,1)S(1)}, bf16[128,960]{0,1:T(8,128)(2,1)}, u32[]{:S(2)}) copy-start(bf16[128,960]{0,1:T(8,128)(2,1)} %param.29) | copy-start | bytes 737284
  188.8 5.6 copy-start.5
  188.8 5.6 copy-start.7
  209.3 48.2 %reduce-scatter.14.cloned.1.call-start = ((), (), s32[]{:S(2)}) async-start(), calls=%async_computation.14 | async-start | bytes 819200 | tf_op jit(solution)/shard_map/reduce_scatter | solution.py:235
  209.4 50.7 %copy-start.18 = (bf16[128,5,3,64]{0,3,2,1:T(8,128)(2,1)S(1)}, bf16[128,5,3,64]{0,3,2,1:T(8,128)(2,1)}, u32[]{:S(2)}) copy-start(bf16[128,5,3,64]{0,3,2,1:T(8,128)(2,1)} %copy-done.17) | copy-start | bytes 737284
  210.2 78.1 %reduce-scatter.30.cloned.1.call-start = ((), (), s32[]{:S(2)}) async-start(), calls=%async_computation.22 | async-start | bytes 1843200
  232.9 29.8 %copy-start.26 = (bf16[128,5,64]{0,2,1:T(8,128)(2,1)}, bf16[128,5,64]{0,2,1:T(8,128)(2,1)S(1)}, u32[]{:S(2)}) copy-start(bf16[128,5,64]{0,2,1:T(8,128)(2,1)S(1)} %convert_element_type.102) | copy-start | bytes 245764
  234.4 84.7 %reduce-scatter.28.cloned.1.call-start = ((), (), s32[]{:S(2)}) async-start(), calls=%async_computation.21 | async-start | bytes 1843200
  260.0 104.5 %reduce-scatter.20.cloned.1.call-start = ((), (), s32[]{:S(2)}) async-start(), calls=%async_computation.17 | async-start | bytes 4915200 | tf_op jit(solution)/shard_map/reduce_scatter | solution.py:271
  262.7 147.3 %reduce-scatter.18.cloned.1.call-start = ((), (), s32[]{:S(2)}) async-start(), calls=%async_computation.16 | async-start | bytes 4915200 | tf_op jit(solution)/shard_map/reduce_scatter | solution.py:268
  266.3 227.3 %reduce-scatter.26.cloned.1.call-start = ((), (), s32[]{:S(2)}) async-start(), calls=%async_computation.20 | async-start | bytes 12288000 | tf_op jit(solution)/shard_map/reduce_scatter | solution.py:275
  271.6 305.7 %reduce-scatter.24.cloned.1.call-start = ((), (), s32[]{:S(2)}) async-start(), calls=%async_computation.19 | async-start | bytes 12288000 | tf_op jit(solution)/shard_map/reduce_scatter | solution.py:274
  277.8 383.0 %reduce-scatter.22.cloned.1.call-start = ((), (), s32[]{:S(2)}) async-start(), calls=%async_computation.18 | async-start | bytes 12288000 | tf_op jit(solution)/shard_map/reduce_scatter | solution.py:273
  284.0 701.2 %all-reduce.10.cloned.1.call-start = ((), (), s32[]{:S(2)}) async-start(), calls=%async_computation.23 | async-start | bytes 19988480 | tf_op jit(solution)/shard_map/psum | solution.py:265
  660.8 5.9 copy-start.12
  660.8 5.9 copy-start.27
  661.6 5.6 copy-start.2
  661.6 5.6 copy-start.20
  985.3 8.2 copy-start.16
  989.4 5.6 copy-start.15
  (18 other events, 54.0 us)
Sparse Core Ops, SparseCore 0:
  9.6 28.0 all-gather.8
  39.3 24.2 all-gather.10
  65.1 38.1 all-gather.14
  104.7 38.5 all-gather.12
  144.8 38.5 all-gather.16
  209.5 22.4 reduce-scatter.15
  235.0 22.4 reduce-scatter.13
  260.6 27.5 reduce-scatter.29
  291.6 27.5 reduce-scatter.27
  321.5 42.8 reduce-scatter.19
  367.2 42.8 reduce-scatter.17
  412.6 80.9 reduce-scatter.25
  496.2 80.9 reduce-scatter.23
  579.7 80.9 reduce-scatter.21
  666.8 318.4 all-reduce.9
where the time goes:
time: 1010 us; the launch traced here: 1000 us
  waiting for transfers between devices  808 us (80%)
  blocking collectives  77.4 us (8%)
  matrix products  65.9 us (7%)
  local copies, waits for them, and re-layouts  27.8 us (3%)
  between operations  15.9 us (2%)
    psum x1, waiting for transfers between devices, local(): lax.psum((lax.psum_scatter(grad_gain_attn, 'shard', scatter_dimension=0,...  287 us
    reduce_scatter x1, waiting for transfers between devices, local(): lax.psum_scatter(grad_w_up, 'shard', scatter_dimension=0, tiled=True)  83.7 us
    reduce_scatter x1, waiting for transfers between devices, local(): lax.psum_scatter(grad_w_down, 'shard', scatter_dimension=0, tiled=True)  83.5 us
    reduce_scatter x1, waiting for transfers between devices, local(): lax.psum_scatter(grad_w_gate, 'shard', scatter_dimension=0, tiled=True)  83.5 us
    reduce_scatter x1, waiting for transfers between devices, local(): lax.psum_scatter(grad_w_query, 'shard', scatter_dimension=0, tiled=True)  45.6 us
    reduce_scatter x1, waiting for transfers between devices, local(): lax.psum_scatter(grad_w_out, 'shard', scatter_dimension=0, tiled=True)  43.4 us
    unnamed x17, waiting for transfers between devices  36.2 us
    all_gather x1, waiting for transfers between devices, local(): lax.all_gather(w_gate, 'shard', axis=0, tiled=True)  35.7 us
  transfers between devices with their start and end apart: 15, of which 13 were waited for; matrix products, arithmetic and copies ran while one was open for 6% of the time, Pallas kernels for 0%

commit v1 on v0

v1 whole, which is shorter than its diff:
```python
import functools
import math

import jax
import jax.numpy as jnp
from jax import lax
from jax.experimental import pallas as pl
from jax.experimental.pallas import tpu as pltpu
from jax.sharding import PartitionSpec as P

H = 15
KV = 5
HD = 64

EPS = 1e-05
THETA = 100000.0
NEG = -1e30
MESH = pl.DeviceIdType.MESH
BF = jnp.bfloat16
F32 = jnp.float32


def rope_tables(positions, head_size):
    half_size = head_size // 2
    frequency = THETA ** (-(jnp.arange(half_size, dtype=F32) * 2.0 / head_size))
    angles = positions.astype(F32)[:, None] * frequency[None, :]
    return (jnp.cos(angles), jnp.sin(angles))


def rotate(values, cosine, sine, direction):
    half_size = values.shape[-1] // 2
    first_half = values[..., :half_size]
    second_half = values[..., half_size:]
    cos_table = cosine[:, None, :]
    sin_table = sine[:, None, :] * direction
    return jnp.concatenate(
        [
            first_half * cos_table - second_half * sin_table,
            second_half * cos_table + first_half * sin_table,
        ],
        axis=-1,
    )


def norm_forward(values, gain):
    inverse = lax.rsqrt(jnp.mean(values * values, axis=-1, keepdims=True) + EPS)
    return (values * inverse * gain, inverse)


def norm_backward(values, inverse, gain, upstream):
    scaled = upstream * gain
    grad_gain = jnp.sum(upstream * values * inverse, axis=0)
    inner = jnp.mean(scaled * values, axis=-1, keepdims=True)
    return (inverse * scaled - values * inverse * inverse * inverse * inner, grad_gain)


def dot(a, b):
    return jnp.dot(a, b, preferred_element_type=F32)


def exchange_kernel(n, n_gather, n_scatter, *refs):
    total = n_gather + n_scatter
    ins, outs = refs[:total], refs[total : 2 * total]
    local_sem, send_sem, recv_sem = refs[2 * total :]
    me = lax.axis_index("shard")
    chips = n // 2
    chip, core = me // 2, me % 2
    mate = 2 * chip + (1 - core)

    barrier = pltpu.get_barrier_semaphore()
    for d in range(1, n):
        pl.semaphore_signal(
            barrier, inc=1, device_id={"shard": (me + d) % n}, device_id_type=MESH
        )
    pl.semaphore_wait(barrier, n - 1)

    count = [0]

    def remote(src, dst, to):
        i = count[0]
        count[0] += 1
        copy = pltpu.make_async_remote_copy(
            src_ref=src,
            dst_ref=dst,
            send_sem=send_sem.at[i],
            recv_sem=recv_sem.at[i],
            device_id={"shard": to},
            device_id_type=MESH,
        )
        copy.start()
        return copy

    pending = []
    far = []
    for a in range(n_gather):
        for k in range(1, chips):
            peer = 2 * ((chip + k) % chips) + core
            far.append((a, k, remote(ins[a], outs[a].at[me], peer)))
    for a in range(n_gather, total):
        for d in range(1, n):
            peer = (me + d) % n
            pending.append(remote(ins[a].at[peer], outs[a].at[me], peer))
    for a in range(n_gather):
        pending.append(remote(ins[a], outs[a].at[me], mate))
    own = []
    for a in range(total):
        src = ins[a] if a < n_gather else ins[a].at[me]
        copy = pltpu.make_async_copy(src, outs[a].at[me], local_sem.at[a])
        copy.start()
        own.append(copy)
    for a, k, copy in far:
        copy.wait_recv()
        origin = 2 * ((chip + chips - k) % chips) + core
        pending.append(remote(outs[a].at[origin], outs[a].at[origin], mate))
    for _, _, copy in far:
        copy.wait_send()
    for copy in pending:
        copy.wait()
    for copy in own:
        copy.wait()


def exchange(n, cid, gathers, scatters):
    chips = n // 2
    g, s = len(gathers), len(scatters)
    copies = g * (2 * (chips - 1) + 1) + s * (n - 1)
    shapes = [jax.ShapeDtypeStruct((n,) + a.shape, a.dtype) for a in gathers]
    shapes += [jax.ShapeDtypeStruct(a.shape, a.dtype) for a in scatters]
    out = pl.pallas_call(
        functools.partial(exchange_kernel, n, g, s),
        out_shape=shapes,
        in_specs=[pl.BlockSpec(memory_space=pl.ANY)] * (g + s),
        out_specs=[pl.BlockSpec(memory_space=pl.ANY)] * (g + s),
        scratch_shapes=[
            pltpu.SemaphoreType.DMA((g + s,)),
            pltpu.SemaphoreType.DMA((copies,)),
            pltpu.SemaphoreType.DMA((copies,)),
        ],
        compiler_params=pltpu.CompilerParams(collective_id=cid, has_side_effects=True),
    )(*gathers, *scatters)
    return out[:g], out[g:]


def rep_sum_kernel(zs, n, *refs):
    ins, outs = refs[:n], refs[n : 2 * n]
    near, sums, others = refs[2 * n : 3 * n], refs[3 * n : 4 * n], refs[4 * n : 5 * n]
    send_sem, recv_sem = refs[5 * n :]
    me = lax.axis_index("rep")
    side, place = me % 2, me // 2
    partner = 2 * place + (1 - side)

    barrier = pltpu.get_barrier_semaphore()
    pl.semaphore_signal(barrier, inc=1, device_id={"rep": partner}, device_id_type=MESH)
    for k in range(1, zs):
        peer = 2 * ((place + k) % zs) + side
        pl.semaphore_signal(barrier, inc=1, device_id={"rep": peer}, device_id_type=MESH)
    pl.semaphore_wait(barrier, zs)

    count = [0]

    def remote(src, dst, to):
        i = count[0]
        count[0] += 1
        copy = pltpu.make_async_remote_copy(
            src_ref=src,
            dst_ref=dst,
            send_sem=send_sem.at[i],
            recv_sem=recv_sem.at[i],
            device_id={"rep": to},
            device_id_type=MESH,
        )
        copy.start()
        return copy

    sends = []
    first = [remote(ins[a].at[1 - side], near[a], partner) for a in range(n)]
    second, third, fourth = {}, {}, {}

    def pair_sum(a):
        first[a].wait_recv()

        def body(z, carry):
            sums[a][z] = (ins[a][side, z].astype(F32) + near[a][z].astype(F32)).astype(BF)
            return carry

        lax.fori_loop(0, zs, body, 0)
        second[a] = []
        for k in range(1, zs):
            at = (place + k) % zs
            second[a].append(remote(sums[a].at[at], others[a].at[k - 1], 2 * at + side))

    def line_sum(a):
        for copy in second[a]:
            copy.wait_recv()
        value = sums[a][place].astype(F32)
        for k in range(1, zs):
            value = value + others[a][k - 1].astype(F32)
        outs[a][side, place] = value.astype(BF)
        third[a] = []
        for k in range(1, zs):
            at = (place + k) % zs
            block = outs[a].at[side, place]
            third[a].append(remote(block, block, 2 * at + side))

    def share(a):
        for copy in third[a]:
            copy.wait_recv()
        fourth[a] = remote(outs[a].at[side], outs[a].at[side], partner)

    for t in range(n + 2):
        if t < n:
            pair_sum(t)
        if 0 <= t - 1 < n:
            line_sum(t - 1)
        if 0 <= t - 2 < n:
            share(t - 2)
    for a in range(n):
        first[a].wait_send()
        for copy in second[a]:
            copy.wait_send()
        for copy in third[a]:
            copy.wait_send()
        fourth[a].wait()


def rep_sum(reps, cid, arrays):
    zs = reps // 2
    n = len(arrays)
    blocks = [a.reshape(2, zs, a.shape[0] // reps, a.shape[1]) for a in arrays]
    copies = n * (2 + 2 * (zs - 1))
    out = pl.pallas_call(
        functools.partial(rep_sum_kernel, zs, n),
        out_shape=[jax.ShapeDtypeStruct(b.shape, b.dtype) for b in blocks],
        in_specs=[pl.BlockSpec(memory_space=pltpu.VMEM)] * n,
        out_specs=[pl.BlockSpec(memory_space=pltpu.VMEM)] * n,
        scratch_shapes=[pltpu.VMEM(b.shape[1:], BF) for b in blocks]
        + [pltpu.VMEM(b.shape[1:], BF) for b in blocks]
        + [pltpu.VMEM((zs - 1,) + b.shape[2:], BF) for b in blocks]
        + [pltpu.SemaphoreType.DMA((copies,)), pltpu.SemaphoreType.DMA((copies,))],
        compiler_params=pltpu.CompilerParams(
            collective_id=cid, has_side_effects=True, vmem_limit_bytes=44 * 1024 * 1024
        ),
    )(*blocks)
    return [o.reshape(a.shape) for o, a in zip(out, arrays)]


def local(
    n,
    reps,
    hidden_in,
    segment_ids,
    positions,
    norm_attn,
    w_query,
    w_key,
    w_value,
    w_out,
    norm_mlp,
    w_gate,
    w_up,
    w_down,
    grad_out,
):
    tok_rows, width = hidden_in.shape
    row_len = tok_rows * n
    first_row = lax.axis_index("shard") * tok_rows
    groups = H // KV
    score_scale = 1.0 / math.sqrt(HD)
    query_idx = first_row + jnp.arange(tok_rows, dtype=jnp.int32)

    gains = jnp.pad(jnp.stack([norm_attn, norm_mlp]), ((0, 14), (0, 0)))
    seg8 = jnp.broadcast_to(segment_ids[None, :], (8, tok_rows))
    got, _ = exchange(
        n, 0, [seg8, gains, w_query, w_key, w_value, w_out, w_gate, w_up, w_down], []
    )
    row_segments = got[0][:, 0, :].reshape(row_len)
    gain_attn = got[1][:, 0, :].reshape(width).astype(F32)
    gain_mlp = got[1][:, 1, :].reshape(width).astype(F32)
    wq, wk, wv, wo, wg, wu, wd = [w.reshape(-1, w.shape[-1]) for w in got[2:]]

    key_idx = jnp.arange(row_len, dtype=jnp.int32)
    allowed = (
        (segment_ids[:, None] == row_segments[None, :])
        & (key_idx[None, :] <= query_idx[:, None])
    )[:, None, None, :]

    resid = hidden_in.astype(F32)
    normed, inv_attn = norm_forward(resid, gain_attn)
    normed_b = normed.astype(BF)
    cos_table, sin_table = rope_tables(positions, HD)
    query = dot(normed_b, wq).reshape(tok_rows, H, HD)
    query_b = rotate(query, cos_table, sin_table, 1.0).astype(BF)
    keys = dot(normed_b, wk).reshape(tok_rows, KV, HD)
    key_b = rotate(keys, cos_table, sin_table, 1.0).astype(BF)
    value_b = dot(normed_b, wv).astype(BF)
    query4 = query_b.reshape(tok_rows, KV, groups, HD)
    (kv_row,), _ = exchange(
        n, 1, [jnp.concatenate([key_b.reshape(tok_rows, KV * HD), value_b], axis=1)], []
    )
    kv_row = kv_row.reshape(row_len, 2, KV, HD)
    key_row, value_row = kv_row[:, 0], kv_row[:, 1]

    scores = (
        jnp.einsum("tgrd,jgd->tgrj", query4, key_row, preferred_element_type=F32) * score_scale
    )
    scores = jnp.where(allowed, scores, NEG)
    row_max = jnp.max(scores, axis=-1)
    weights = jnp.where(allowed, jnp.exp(scores - row_max[..., None]), 0.0)
    row_sum = jnp.sum(weights, axis=-1)
    probs = weights / row_sum[..., None]
    probs_b = probs.astype(BF)
    accum = jnp.einsum("tgrj,jgd->tgrd", probs_b, value_row, preferred_element_type=F32)
    attn4 = accum.astype(BF)
    attn_b = attn4.reshape(tok_rows, H * HD)
    mixed = resid + dot(attn_b, wo)
    normed_mlp, inv_mlp = norm_forward(mixed, gain_mlp)
    normed_mlp_b = normed_mlp.astype(BF)
    gate = dot(normed_mlp_b, wg)
    upper = dot(normed_mlp_b, wu)
    sigma = jax.nn.sigmoid(gate)
    act_b = (gate * sigma * upper).astype(BF)
    result = (mixed + dot(act_b, wd)).astype(BF)

    grad_act = dot(grad_out, wd.T)
    grad_gate_b = (grad_act * upper * sigma * (1.0 + gate * (1.0 - sigma))).astype(BF)
    grad_up_b = (grad_act * gate * sigma).astype(BF)
    grad_normed_mlp = dot(grad_gate_b, wg.T) + dot(grad_up_b, wu.T)
    grad_mixed_n, grad_gain_mlp = norm_backward(mixed, inv_mlp, gain_mlp, grad_normed_mlp)
    grad_mixed = grad_out.astype(F32) + grad_mixed_n
    grad_mixed_b = grad_mixed.astype(BF)
    grad_attn_b = dot(grad_mixed_b, wo.T).astype(BF)
    grad_attn4 = grad_attn_b.reshape(tok_rows, KV, groups, HD)
    delta = jnp.sum(grad_attn4.astype(F32) * attn4.astype(F32), axis=-1)

    value_part = jnp.einsum("tgrj,tgrd->jgd", probs_b, grad_attn4, preferred_element_type=F32)
    grad_probs = jnp.einsum("tgrd,jgd->tgrj", grad_attn4, value_row, preferred_element_type=F32)
    grad_scores = (probs * (grad_probs - delta[..., None])).astype(BF)
    grad_query = (
        jnp.einsum("tgrj,jgd->tgrd", grad_scores, key_row, preferred_element_type=F32)
        * score_scale
    )
    key_part = (
        jnp.einsum("tgrj,tgrd->jgd", grad_scores, query4, preferred_element_type=F32)
        * score_scale
    )
    parts = jnp.concatenate(
        [key_part.reshape(row_len, KV * HD), value_part.reshape(row_len, KV * HD)], axis=1
    )
    _, (parts,) = exchange(n, 2, [], [parts.astype(BF).reshape(n, tok_rows, 2 * KV * HD)])
    own = jnp.sum(parts.astype(F32), axis=0)
    own_keys = own[:, : KV * HD].reshape(tok_rows, KV, HD)
    grad_query_b = (
        rotate(grad_query.reshape(tok_rows, H, HD), cos_table, sin_table, -1.0)
        .astype(BF)
        .reshape(tok_rows, H * HD)
    )
    grad_key_b = (
        rotate(own_keys, cos_table, sin_table, -1.0).astype(BF).reshape(tok_rows, KV * HD)
    )
    grad_value_b = own[:, KV * HD :].astype(BF)
    grad_normed = dot(grad_query_b, wq.T) + dot(grad_key_b, wk.T) + dot(grad_value_b, wv.T)
    grad_resid_n, grad_gain_attn = norm_backward(resid, inv_attn, gain_attn, grad_normed)
    grad_hidden = grad_mixed + grad_resid_n

    gain_sums = lax.psum(jnp.stack([grad_gain_attn, grad_gain_mlp]), ("rep", "shard"))
    rows = width // n
    gain_own = lax.dynamic_slice_in_dim(gain_sums, lax.axis_index("shard") * rows, rows, 1)

    def sliced(x):
        return x.reshape(tok_rows, n, -1).transpose(1, 0, 2)

    right_small = jnp.concatenate([grad_query_b, grad_key_b, grad_value_b, grad_mixed_b], axis=1)
    (g_gate, g_up, g_small, g_out), (x_attn, x_ctx, x_mlp, x_act) = exchange(
        n,
        3,
        [grad_gate_b, grad_up_b, right_small, grad_out],
        [sliced(normed_b), sliced(attn_b), sliced(normed_mlp_b), sliced(act_b)],
    )

    def padded(x):
        size = x.shape[-1]
        full = -(-size // (16 * reps)) * (16 * reps)
        return jnp.pad(x.reshape(row_len, size), ((0, 0), (0, full - size)))

    def product(x, g):
        return dot(padded(x).T, g.reshape(row_len, -1)).astype(BF)

    g_small = g_small.reshape(row_len, -1)
    cut = H * HD + 2 * KV * HD
    small = jnp.concatenate(
        [product(x_attn, g_small[:, :cut]), product(x_ctx, g_small[:, cut:])], axis=1
    )
    t_gate, t_up, t_small, t_down = rep_sum(
        reps, 4, [product(x_mlp, g_gate), product(x_mlp, g_up), small, product(x_act, g_out)]
    )
    t_small = t_small[:rows].astype(F32)
    q, k = H * HD, KV * HD
    return (
        result,
        grad_hidden,
        gain_own[0],
        t_small[:, :q],
        t_small[:, q : q + k],
        t_small[:, q + k : q + 2 * k],
        t_small[:, q + 2 * k :],
        gain_own[1],
        t_gate[:rows].astype(F32),
        t_up[:rows].astype(F32),
        t_down[: w_down.shape[0]].astype(F32),
    )


def solution(mesh):
    both = P(("rep", "shard"), None)
    tokens = P(("rep", "shard"))
    vector = P("shard")
    matrix = P("shard", None)
    return jax.shard_map(
        functools.partial(local, mesh.shape["shard"], mesh.shape["rep"]),
        mesh=mesh,
        in_specs=(both, tokens, tokens, vector, matrix, matrix, matrix, matrix, vector)
        + (matrix, matrix, matrix, both),
        out_specs=(both, both, vector, matrix, matrix, matrix, matrix, vector)
        + (matrix, matrix, matrix),
        check_vma=False,
    )
```

time: 1010 us -> 575 us (0.57)
  waiting for transfers between devices: 808 us -> 0 us
  Pallas kernels: 0 us -> 412 us
  blocking collectives: 77.4 us -> 43.8 us
  local copies, waits for them, and re-layouts: 27.8 us -> 44.5 us
  between operations: 15.9 us -> 1.61 us
  matrix products: 65.9 us -> 51.8 us
  other arithmetic: 8.81 us -> 20 us
    pallas_call x0 -> x5, Pallas kernels: none -> 412 us  [the longest x4 259 us: exchange(): pl.pallas_call(functools.partial(exchange_kernel, n, g, s), out_shape=sha...]
    reduce_scatter x7 -> x0, waiting for transfers between devices: 384 us -> none  [the longest x1 83.7 us: local(): lax.psum_scatter(grad_w_up, 'shard', scatter_dimension=0, tiled=True)]
    psum x1 -> x0, waiting for transfers between devices: 287 us -> none  [local(): lax.psum((lax.psum_scatter(grad_gain_attn, 'shard', scatter_dimension=0,...]
    all_gather x5 -> x0, waiting for transfers between devices: 99.7 us -> none  [the longest x1 35.7 us: local(): lax.all_gather(w_gate, 'shard', axis=0, tiled=True)]
    all_gather x5 -> x0, blocking collectives: 40.2 us -> none  [the longest x1 11.4 us: local(): lax.all_gather(w_key, 'shard', axis=0, tiled=True)]
    unnamed x17 -> x0, waiting for transfers between devices: 36.2 us -> none
    psum x1, blocking collectives: 23 us -> 43.8 us  [local(): lax.psum(jnp.stack([grad_gain_attn, grad_gain_mlp]), ('rep', 'shard'))]
    dot_general x26 -> x24, matrix products: 62.9 us -> 48.3 us  [the longest x19 40 us: dot(): return jnp.dot(a, b, preferred_element_type=F32)]
  transfers between devices with their start and end apart: 15 -> 0, of which waited for: 13 -> 0; matrix products, arithmetic and copies ran while one was open for 6% -> 0% of each run, Pallas kernels for 0% -> 0%
where the time goes in v1:
time: 575 us; the launch traced here: 574 us
  Pallas kernels  412 us (72%)
  matrix products  51.8 us (9%)
  local copies, waits for them, and re-layouts  44.5 us (8%)
  blocking collectives  43.8 us (8%)
  other arithmetic  20 us (3%)
    pallas_call x4, Pallas kernels, exchange(): pl.pallas_call(functools.partial(exchange_kernel, n, g, s), out_shape=sha...  259 us
    pallas_call x1, Pallas kernels, rep_sum(): pl.pallas_call(functools.partial(rep_sum_kernel, zs, n), out_shape=[jax.S...  153 us
    psum x1, blocking collectives, local(): lax.psum(jnp.stack([grad_gain_attn, grad_gain_mlp]), ('rep', 'shard'))  43.8 us
    dot_general x19, matrix products, dot(): return jnp.dot(a, b, preferred_element_type=F32)  40 us
    unnamed x124, local copies, waits for them, and re-layouts  16.7 us

profile of v1, /device:TPU:0, one launch (start us, length us, event | category | flops | bytes accessed | tf_op | source)
XLA Modules:
  0.0 573.6 jit_solution(7269897048828463924)
XLA Ops:
  0.7 2.5 copy.112.refs_8_
  6.1 160.1 %shard_map.212 = (s32[4,8,128]{2,1,0:T(8,128)}, bf16[4,16,240]{2,1,0:T(8,128)(2,1)}, bf16[4,240,960]{2,1,0:T(8,128)(2,1)}, bf16[4,240,320]{2,1,0:T(8,128)(2,1)},...) custom-call(s32[8,128]{1,0:T(8,128)} %broadcast_in_dim.16.refs_0_, ...), custom_call_target="tpu_custom_call" | custom-call | tf_op jit(solution)/shard_map/pallas_call | solution.py:129
  171.6 8.3 %shard_map.213 = bf16[4,128,640]{2,1,0:T(8,128)(2,1)} custom-call(bf16[128,640]{1,0:T(8,128)(2,1)} %pad_maximum_fusion.3.refs_0_), custom_call_target="tpu_custom_call" | custom-call | tf_op jit(solution)/shard_map/pallas_call | solution.py:129
  179.9 2.1 copy.117
  182.1 2.2 reshape.318
  184.3 2.4 copy.118
  186.7 2.3 fusion.30
  190.0 3.4 fusion.58
  193.5 2.6 fusion.8
  198.5 3.4 fusion.62
  203.2 6.1 %multiply_convert_fusion = (bf16[128,2560]{1,0:T(8,128)(2,1)S(1)}, bf16[128,2560]{1,0:T(8,128)(2,1)S(1)}, bf16[128,2560]{1,0:T(8,128)(2,1)}) fusion(f32[128,2560]{1,0:T(8,128)S(1)} %fusion.61, f32[128,2560]{1,0:T(8,128)S(1)} %fusion.62, bf16[2560,960]{1,0:T(8,128)(2,1)} %bitcast.188, bf16[128,960]{0,1:T(8,128)(2,1)S(1)} %copy-done.32), kind=kOutput, calls=%fused_computation.21 | convolution fusion | flops 634388480 | bytes 9748480 | tf_op jit(solution)/shard_map/dot_general | solution.py:58
  211.0 3.1 multiply_reduce_fusion
  217.2 2.3 convolution_convert_fusion.4
  224.7 3.1 fusion.14
  229.6 1.9 copy.130
  231.6 2.4 fusion.15
  235.5 2.0 pad_maximum_fusion.1.refs_0_
  237.6 8.3 %shard_map.214 = bf16[4,128,640]{2,1,0:T(8,128)(2,1)} custom-call(bf16[4,128,640]{2,1,0:T(8,128)(2,1)} %pad_maximum_fusion.1.refs_0_), custom_call_target="tpu_custom_call" | custom-call | tf_op jit(solution)/shard_map/pallas_call | solution.py:129
  253.1 82.0 %shard_map.215 = (bf16[4,128,2560]{2,1,0:T(8,128)(2,1)}, bf16[4,128,2560]{2,1,0:T(8,128)(2,1)}, bf16[4,128,2560]{2,1,0:T(8,128)(2,1)}, bf16[4,128,960]{2,1,0:T(8...) custom-call(bf16[128,2560]{1,0:T(8,128)(2,1)} %copy-done.13, ...), custom_call_target="tpu_custom_call" | custom-call | tf_op jit(solution)/shard_map/pallas_call | solution.py:129
  335.1 2.4 bitcast_convert_fusion
  337.5 1.9 copy.148
  339.5 2.3 convolution_convert_fusion.2
  341.7 2.3 convolution_convert_fusion.3
  345.0 2.8 convolution_convert_fusion
  348.7 153.3 %shard_map.216 = (bf16[2,4,32,2560]{3,2,1,0:T(8,128)(2,1)S(1)}, bf16[2,4,32,2560]{3,2,1,0:T(8,128)(2,1)S(1)}, bf16[2,4,32,2560]{3,2,1,0:T(8,128)(2,1)S(1)}, bf16[2,4,80,960]{3,2,1,0:T(8,128)(2,1)S(1)}) custom-call(bf16[2,4,32,2560]{3,2,1,0:T(8,128)(2,1)S(1)} %bitcast.170, bf16[2,4,32,2560]{3,2,1,0:T(8,128)(2,1)S(1)} %bitcast.169, ...), custom_call_target="tpu_custom_call" | custom-call | tf_op jit(solution)/shard_map/pallas_call | solution.py:231
  502.1 2.9 slice_convert_fusion
  504.9 1.9 bitcast_convert_fusion.1
  506.8 3.2 copy.153
  512.9 2.0 copy.151
  519.8 2.1 fusion.27
  521.9 43.8 %psum.7 = f32[2,960]{1,0:T(2,128)S(1)} all-reduce(f32[2,960]{1,0:T(2,128)S(1)} %pad_maximum_fusion.10), channel_id=1, replica_groups=mesh['rep'=8,'shard'=4] {'rep','shard'}, use_global_device_ids=true, to_apply=%region_10.11 | all-reduce | flops 1920 | bytes 15360 | tf_op jit(solution)/shard_map/psum | solution.py:365
  569.5 3.3 fusion.13
  (192 shorter events, 47.0 us)
Async XLA Ops:
  0.7 3.4 copy-start.34
  0.7 4.2 copy-start.50
  0.7 4.2 copy-start.51
  0.7 4.8 copy-start.47
  6.1 161.0 %copy-start.31 = (bf16[128,960]{0,1:T(8,128)(2,1)S(1)}, bf16[128,960]{0,1:T(8,128)(2,1)}, u32[]{:S(2)}) copy-start(bf16[128,960]{0,1:T(8,128)(2,1)} %param.13) | copy-start | bytes 737284
  166.2 3.1 copy-start.52
  170.7 13.6 %copy-start = (bf16[4,240,960]{2,1,0:T(8,128)(2,1)S(1)}, bf16[4,240,960]{2,1,0:T(8,128)(2,1)}, u32[]{:S(2)}) copy-start(bf16[4,240,960]{2,1,0:T(8,128)(2,1)} %get-tuple-element.36) | copy-start | bytes 5529604
  186.7 3.3 copy-start.17
  189.0 4.4 copy-start.29
  189.1 4.4 copy-start.30
  198.3 12.6 %copy-start.43 = (f32[128]{0:T(128)}, f32[128]{0:T(128)S(1)}, u32[]{:S(2)}) copy-start(f32[128]{0:T(128)S(1)} %add_rsqrt_fusion) | copy-start | bytes 1540
  198.4 12.6 %copy-start.36 = (f32[960]{0:T(1024)}, f32[960]{0:T(1024)S(1)}, u32[]{:S(2)}) copy-start(f32[960]{0:T(1024)S(1)} %reshape.345) | copy-start | bytes 11524
  198.4 3.7 slice-start.2
  198.5 3.7 slice-start.3
  202.3 8.7 %slice-start = ((s8[4915200]{0:T(1024)(128)(4,1)}), s8[4194304]{0:T(1024)(128)(4,1)S(1)}, s32[]{:S(2)}) async-start(s8[4915200]{0:T(1024)(128)(4,1)} %bitcast.175), calls=%async_computation | async-start | bytes 8388608
  203.2 7.8 %slice-start.1 = ((s8[4915200]{0:T(1024)(128)(4,1)}), s8[720896]{0:T(1024)(128)(4,1)S(1)}, s32[]{:S(2)}) async-start(s8[4915200]{0:T(1024)(128)(4,1)} %bitcast.175), calls=%async_computation.1 | async-start | bytes 1441792
  215.7 3.8 copy-start.5
  215.7 4.9 copy-start.7
  215.7 4.9 copy-start.42
  219.5 3.1 copy-start.24
  223.9 7.7 %copy-start.22 = (bf16[128,15,64]{0,2,1:T(8,128)(2,1)}, bf16[128,15,64]{0,2,1:T(8,128)(2,1)S(1)}, u32[]{:S(2)}) copy-start(bf16[128,15,64]{0,2,1:T(8,128)(2,1)S(1)} %maximum_convert_fusion) | copy-start | bytes 737284
  237.6 10.0 %copy-start.21 = (bf16[128,960]{1,0:T(8,128)(2,1)S(1)}, bf16[128,960]{1,0:T(8,128)(2,1)}, u32[]{:S(2)}) copy-start(bf16[128,960]{1,0:T(8,128)(2,1)} %copy-done.20) | copy-start | bytes 737284
  237.6 10.1 %copy-start.27 = (bf16[128,960]{1,0:T(8,128)(2,1)S(1)}, bf16[128,960]{1,0:T(8,128)(2,1)}, u32[]{:S(2)}) copy-start(bf16[128,960]{1,0:T(8,128)(2,1)} %copy.136) | copy-start | bytes 737284
  511.9 6.5 %copy-start.11 = (bf16[4,240,320]{2,1,0:T(8,128)(2,1)S(1)}, bf16[4,240,320]{2,1,0:T(8,128)(2,1)}, u32[]{:S(2)}) copy-start(bf16[4,240,320]{2,1,0:T(8,128)(2,1)} %get-tuple-element.34) | copy-start | bytes 1843204
  512.9 6.8 %copy-start.1 = (bf16[4,240,960]{2,1,0:T(8,128)(2,1)S(1)}, bf16[4,240,960]{2,1,0:T(8,128)(2,1)}, u32[]{:S(2)}) copy-start(bf16[4,240,960]{2,1,0:T(8,128)(2,1)} %get-tuple-element.36) | copy-start | bytes 5529604
  512.9 6.8 %copy-start.39 = (f32[960]{0:T(1024)S(1)}, f32[960]{0:T(1024)}, u32[]{:S(2)}) copy-start(f32[960]{0:T(1024)} %copy-done.38) | copy-start | bytes 11524
  512.9 6.8 %copy-start.46 = (f32[128]{0:T(128)S(1)}, f32[128]{0:T(128)}, u32[]{:S(2)}) copy-start(f32[128]{0:T(128)} %copy-done.45) | copy-start | bytes 1540
  519.8 47.3 %copy-start.4 = (f32[128,960]{1,0:T(8,128)S(1)}, f32[128,960]{1,0:T(8,128)}, u32[]{:S(2)}) copy-start(f32[128,960]{1,0:T(8,128)} %get-tuple-element.116) | copy-start | bytes 1474564
  519.8 47.3 %copy-start.6 = (bf16[128,960]{1,0:T(8,128)(2,1)S(1)}, bf16[128,960]{1,0:T(8,128)(2,1)}, u32[]{:S(2)}) copy-start(bf16[128,960]{1,0:T(8,128)(2,1)} %copy-done.5) | copy-start | bytes 737284
  519.8 47.3 %copy-start.37 = (f32[960]{0:T(1024)S(1)}, f32[960]{0:T(1024)}, u32[]{:S(2)}) copy-start(f32[960]{0:T(1024)} %copy-done.36) | copy-start | bytes 11524
  519.8 47.2 %copy-start.44 = (f32[128]{0:T(128)S(1)}, f32[128]{0:T(128)}, u32[]{:S(2)}) copy-start(f32[128]{0:T(128)} %copy-done.43) | copy-start | bytes 1540
  521.9 47.6 %copy-start.15 = (bf16[128,2560]{1,0:T(8,128)(2,1)S(1)}, bf16[128,2560]{1,0:T(8,128)(2,1)}, u32[]{:S(2)}) copy-start(bf16[128,2560]{1,0:T(8,128)(2,1)} %get-tuple-element.94) | copy-start | bytes 1966084
  (25 other events, 54.2 us)

commit v2 on v1

--- a/solution.py
+++ b/solution.py
@@ -141,10 +141,162 @@
     return out[:g], out[g:]
 
 
+def weight_kernel(n, n_small, axes, *refs):
+    n_big = len(axes)
+    total = n_small + n_big
+    ins, outs = refs[:total], refs[total : 2 * total]
+    local_sem, send_sem, recv_sem = refs[2 * total :]
+    me, rep = lax.axis_index("shard"), lax.axis_index("rep")
+    chips = n // 2
+    chip, core = me // 2, me % 2
+    mate = {"shard": 2 * chip + (1 - core)}
+    near_a = {"rep": rep + 1 - 2 * (rep % 2)}
+    near_b = {"rep": rep + 2 - 4 * ((rep // 2) % 2)}
+    own_q = rep % 4
+    quarter_b, quarter_d = (own_q + 2) % 4, 3 - own_q
+    quarter_a = own_q + 1 - 2 * (own_q % 2)
+
+    barrier = pltpu.get_barrier_semaphore()
+    for d in range(1, n):
+        pl.semaphore_signal(
+            barrier, inc=1, device_id={"shard": (me + d) % n}, device_id_type=MESH
+        )
+    for there in (near_a, near_b):
+        pl.semaphore_signal(barrier, inc=1, device_id=there, device_id_type=MESH)
+    pl.semaphore_wait(barrier, n + 1)
+
+    count = [0]
+
+    def remote(src, dst, to):
+        i = count[0]
+        count[0] += 1
+        copy = pltpu.make_async_remote_copy(
+            src_ref=src,
+            dst_ref=dst,
+            send_sem=send_sem.at[i],
+            recv_sem=recv_sem.at[i],
+            device_id=to,
+            device_id_type=MESH,
+        )
+        copy.start()
+        return copy
+
+    def piece(ref, a, which, part=None):
+        axis = axes[a - n_small]
+        unit = 16 if axis == 0 else 128
+        size = ins[a].shape[axis] // 4
+        lo = (size // unit) * 2 // 5 * unit
+        first, length = {None: (0, size), 0: (0, lo), 1: (lo, size - lo)}[part]
+        at = pl.ds(pl.multiple_of(which * size + first, unit), length)
+        return ref.at[at, :] if axis == 0 else ref.at[:, at]
+
+    waits = []
+    received = []
+
+    def to_mate(ref):
+        waits.append(remote(ref, ref, mate))
+
+    def arrived(copy):
+        copy.wait_recv()
+        received.append(copy)
+
+    direct, side_a, side_b, corner_x, corner_a, plain = {}, {}, {}, {}, {}, []
+    for a in range(n_small):
+        for k in range(1, chips):
+            peer = {"shard": 2 * ((chip + k) % chips) + core}
+            plain.append((a, k, remote(ins[a], outs[a].at[me], peer)))
+        waits.append(remote(ins[a], outs[a].at[me], mate))
+    for a in range(n_small, total):
+        for k in range(1, chips):
+            peer = {"shard": 2 * ((chip + k) % chips) + core}
+            direct[a, k] = remote(
+                piece(ins[a], a, own_q), piece(outs[a].at[me], a, own_q), peer
+            )
+    for a in range(n_small, total):
+        for k in range(1, chips):
+            peer = {"shard": 2 * ((chip + k) % chips) + core}
+            corner_x[a, k] = remote(
+                piece(ins[a], a, quarter_d, 0), piece(outs[a].at[me], a, quarter_d, 0), peer
+            )
+        waits.append(remote(ins[a], outs[a].at[me], mate))
+    own = []
+    for a in range(total):
+        copy = pltpu.make_async_copy(ins[a], outs[a].at[me], local_sem.at[a])
+        copy.start()
+        own.append(copy)
+
+    def origin(k):
+        return 2 * ((chip + chips - k) % chips) + core
+
+    def spread(a):
+        for k in range(1, chips):
+            arrived(direct[a, k])
+            block = piece(outs[a].at[origin(k)], a, own_q)
+            side_a[a, k] = remote(block, block, near_a)
+            side_b[a, k] = remote(block, block, near_b)
+            to_mate(block)
+
+    def pass_on(a):
+        for k in range(1, chips):
+            arrived(side_b[a, k])
+            slot = outs[a].at[origin(k)]
+            block = piece(slot, a, quarter_b, 1)
+            corner_a[a, k] = remote(block, block, near_a)
+            to_mate(piece(slot, a, quarter_b))
+            arrived(side_a[a, k])
+            to_mate(piece(slot, a, quarter_a))
+
+    def finish(a):
+        for k in range(1, chips):
+            slot = outs[a].at[origin(k)]
+            arrived(corner_x[a, k])
+            to_mate(piece(slot, a, quarter_d, 0))
+            arrived(corner_a[a, k])
+            to_mate(piece(slot, a, quarter_d, 1))
+
+    for t in range(n_big + 2):
+        if t < n_big:
+            spread(n_small + t)
+        if 0 <= t - 1 < n_big:
+            pass_on(n_small + t - 1)
+        if 0 <= t - 2 < n_big:
+            finish(n_small + t - 2)
+    for a, k, copy in plain:
+        arrived(copy)
+        to_mate(outs[a].at[origin(k)])
+    for copy in received:
+        copy.wait_send()
+    for copy in waits:
+        copy.wait()
+    for copy in own:
+        copy.wait()
+
+
+def gather_weights(n, cid, small, big):
+    arrays = list(small) + [a for a, _ in big]
+    chips = n // 2
+    copies = len(small) * (2 * chips - 1) + len(big) * (10 * (chips - 1) + 1)
+    total = len(arrays)
+    return pl.pallas_call(
+        functools.partial(weight_kernel, n, len(small), tuple(axis for _, axis in big)),
+        out_shape=[jax.ShapeDtypeStruct((n,) + a.shape, a.dtype) for a in arrays],
+        in_specs=[pl.BlockSpec(memory_space=pl.ANY)] * total,
+        out_specs=[pl.BlockSpec(memory_space=pl.ANY)] * total,
+        scratch_shapes=[
+            pltpu.SemaphoreType.DMA((total,)),
+            pltpu.SemaphoreType.DMA((copies,)),
+            pltpu.SemaphoreType.DMA((copies,)),
+        ],
+        compiler_params=pltpu.CompilerParams(collective_id=cid, has_side_effects=True),
+    )(*arrays)
+
+
 def rep_sum_kernel(zs, n, *refs):
-    ins, outs = refs[:n], refs[n : 2 * n]
-    near, sums, others = refs[2 * n : 3 * n], refs[3 * n : 4 * n], refs[4 * n : 5 * n]
-    send_sem, recv_sem = refs[5 * n :]
+    gain_in, refs = refs[0], refs[1:]
+    ins, gain_out, refs = refs[:n], refs[n], refs[n + 1 :]
+    outs, near, sums = refs[:n], refs[n : 2 * n], refs[2 * n : 3 * n]
+    others = refs[3 * n : 4 * n]
+    gain_near, gain_pair, gain_all, send_sem, recv_sem = refs[4 * n :]
     me = lax.axis_index("rep")
     side, place = me % 2, me // 2
     partner = 2 * place + (1 - side)
@@ -172,9 +324,16 @@
         copy.start()
         return copy
 
-    sends = []
+    gain_first = remote(gain_in, gain_near, partner)
     first = [remote(ins[a].at[1 - side], near[a], partner) for a in range(n)]
     second, third, fourth = {}, {}, {}
+    gain_first.wait_recv()
+    gain_pair[...] = gain_in[...] + gain_near[...]
+    gain_all[place] = gain_pair[...]
+    gain_second = [
+        remote(gain_pair, gain_all.at[place], 2 * ((place + k) % zs) + side)
+        for k in range(1, zs)
+    ]
 
     def pair_sum(a):
         first[a].wait_recv()
@@ -214,6 +373,13 @@
             line_sum(t - 1)
         if 0 <= t - 2 < n:
             share(t - 2)
+    for copy in gain_second:
+        copy.wait()
+    value = gain_all[0]
+    for z in range(1, zs):
+        value = value + gain_all[z]
+    gain_out[...] = value
+    gain_first.wait_send()
     for a in range(n):
         first[a].wait_send()
         for copy in second[a]:
@@ -223,25 +389,27 @@
         fourth[a].wait()
 
 
-def rep_sum(reps, cid, arrays):
+def rep_sum(reps, cid, gain, arrays):
     zs = reps // 2
     n = len(arrays)
     blocks = [a.reshape(2, zs, a.shape[0] // reps, a.shape[1]) for a in arrays]
-    copies = n * (2 + 2 * (zs - 1))
+    copies = n * (2 + 2 * (zs - 1)) + zs
     out = pl.pallas_call(
         functools.partial(rep_sum_kernel, zs, n),
-        out_shape=[jax.ShapeDtypeStruct(b.shape, b.dtype) for b in blocks],
-        in_specs=[pl.BlockSpec(memory_space=pltpu.VMEM)] * n,
-        out_specs=[pl.BlockSpec(memory_space=pltpu.VMEM)] * n,
+        out_shape=[jax.ShapeDtypeStruct(b.shape, b.dtype) for b in [gain] + blocks],
+        in_specs=[pl.BlockSpec(memory_space=pltpu.VMEM)] * (n + 1),
+        out_specs=[pl.BlockSpec(memory_space=pltpu.VMEM)] * (n + 1),
         scratch_shapes=[pltpu.VMEM(b.shape[1:], BF) for b in blocks]
         + [pltpu.VMEM(b.shape[1:], BF) for b in blocks]
         + [pltpu.VMEM((zs - 1,) + b.shape[2:], BF) for b in blocks]
+        + [pltpu.VMEM(gain.shape, F32)] * 2
+        + [pltpu.VMEM((zs,) + gain.shape, F32)]
         + [pltpu.SemaphoreType.DMA((copies,)), pltpu.SemaphoreType.DMA((copies,))],
         compiler_params=pltpu.CompilerParams(
             collective_id=cid, has_side_effects=True, vmem_limit_bytes=44 * 1024 * 1024
         ),
-    )(*blocks)
-    return [o.reshape(a.shape) for o, a in zip(out, arrays)]
+    )(gain, *blocks)
+    return out[0], [o.reshape(a.shape) for o, a in zip(out[1:], arrays)]
 
 
 def local(
@@ -270,13 +438,31 @@
 
     gains = jnp.pad(jnp.stack([norm_attn, norm_mlp]), ((0, 14), (0, 0)))
     seg8 = jnp.broadcast_to(segment_ids[None, :], (8, tok_rows))
-    got, _ = exchange(
-        n, 0, [seg8, gains, w_query, w_key, w_value, w_out, w_gate, w_up, w_down], []
+    rows = width // n
+
+    def row_pad(x, unit):
+        return jnp.pad(x, ((0, -x.shape[0] % unit), (0, 0)))
+
+    w_small = jnp.concatenate([w_query, w_key, w_value, w_out], axis=1)
+    got = gather_weights(
+        n,
+        0,
+        [seg8, gains],
+        [
+            (row_pad(w_small, 16), 1),
+            (row_pad(w_gate, 16), 1),
+            (row_pad(w_up, 16), 1),
+            (row_pad(w_down, 64), 0),
+        ],
     )
     row_segments = got[0][:, 0, :].reshape(row_len)
     gain_attn = got[1][:, 0, :].reshape(width).astype(F32)
     gain_mlp = got[1][:, 1, :].reshape(width).astype(F32)
-    wq, wk, wv, wo, wg, wu, wd = [w.reshape(-1, w.shape[-1]) for w in got[2:]]
+    ws, wg, wu = [w[:, :rows].reshape(width, -1) for w in got[2:5]]
+    wd = got[5][:, : w_down.shape[0]].reshape(-1, width)
+    q, k = H * HD, KV * HD
+    cut = q + 2 * k
+    wqkv, wo = ws[:, :cut], ws[:, cut:]
 
     key_idx = jnp.arange(row_len, dtype=jnp.int32)
     allowed = (
@@ -288,11 +474,12 @@
     normed, inv_attn = norm_forward(resid, gain_attn)
     normed_b = normed.astype(BF)
     cos_table, sin_table = rope_tables(positions, HD)
-    query = dot(normed_b, wq).reshape(tok_rows, H, HD)
+    qkv = dot(normed_b, wqkv)
+    query = qkv[:, :q].reshape(tok_rows, H, HD)
     query_b = rotate(query, cos_table, sin_table, 1.0).astype(BF)
-    keys = dot(normed_b, wk).reshape(tok_rows, KV, HD)
+    keys = qkv[:, q : q + k].reshape(tok_rows, KV, HD)
     key_b = rotate(keys, cos_table, sin_table, 1.0).astype(BF)
-    value_b = dot(normed_b, wv).astype(BF)
+    value_b = qkv[:, q + k :].astype(BF)
     query4 = query_b.reshape(tok_rows, KV, groups, HD)
     (kv_row,), _ = exchange(
         n, 1, [jnp.concatenate([key_b.reshape(tok_rows, KV * HD), value_b], axis=1)], []
@@ -358,23 +545,23 @@
         rotate(own_keys, cos_table, sin_table, -1.0).astype(BF).reshape(tok_rows, KV * HD)
     )
     grad_value_b = own[:, KV * HD :].astype(BF)
-    grad_normed = dot(grad_query_b, wq.T) + dot(grad_key_b, wk.T) + dot(grad_value_b, wv.T)
+    grad_qkv_b = jnp.concatenate([grad_query_b, grad_key_b, grad_value_b], axis=1)
+    grad_normed = dot(grad_qkv_b, wqkv.T)
     grad_resid_n, grad_gain_attn = norm_backward(resid, inv_attn, gain_attn, grad_normed)
     grad_hidden = grad_mixed + grad_resid_n
 
-    gain_sums = lax.psum(jnp.stack([grad_gain_attn, grad_gain_mlp]), ("rep", "shard"))
-    rows = width // n
-    gain_own = lax.dynamic_slice_in_dim(gain_sums, lax.axis_index("shard") * rows, rows, 1)
+    gain_parts = jnp.stack([grad_gain_attn, grad_gain_mlp]).reshape(2, n, rows)
+    gain_parts = jnp.pad(gain_parts.transpose(1, 0, 2), ((0, 0), (0, 6), (0, 0)))
 
     def sliced(x):
         return x.reshape(tok_rows, n, -1).transpose(1, 0, 2)
 
-    right_small = jnp.concatenate([grad_query_b, grad_key_b, grad_value_b, grad_mixed_b], axis=1)
-    (g_gate, g_up, g_small, g_out), (x_attn, x_ctx, x_mlp, x_act) = exchange(
+    right_small = jnp.concatenate([grad_qkv_b, grad_mixed_b], axis=1)
+    (g_gate, g_up, g_small, g_out), (x_attn, x_ctx, x_mlp, x_act, gain_parts) = exchange(
         n,
         3,
         [grad_gate_b, grad_up_b, right_small, grad_out],
-        [sliced(normed_b), sliced(attn_b), sliced(normed_mlp_b), sliced(act_b)],
+        [sliced(normed_b), sliced(attn_b), sliced(normed_mlp_b), sliced(act_b), gain_parts],
     )
 
     def padded(x):
@@ -386,15 +573,16 @@
         return dot(padded(x).T, g.reshape(row_len, -1)).astype(BF)
 
     g_small = g_small.reshape(row_len, -1)
-    cut = H * HD + 2 * KV * HD
     small = jnp.concatenate(
         [product(x_attn, g_small[:, :cut]), product(x_ctx, g_small[:, cut:])], axis=1
     )
-    t_gate, t_up, t_small, t_down = rep_sum(
-        reps, 4, [product(x_mlp, g_gate), product(x_mlp, g_up), small, product(x_act, g_out)]
+    gain_own, (t_gate, t_up, t_small, t_down) = rep_sum(
+        reps,
+        4,
+        jnp.sum(gain_parts, axis=0),
+        [product(x_mlp, g_gate), product(x_mlp, g_up), small, product(x_act, g_out)],
     )
     t_small = t_small[:rows].astype(F32)
-    q, k = H * HD, KV * HD
     return (
         result,
         grad_hidden,

time: 575 us -> 519 us (0.903)
  blocking collectives: 43.8 us -> 0 us
    pallas_call x4 -> x3, Pallas kernels: 259 us -> 100 us  [exchange(): pl.pallas_call(functools.partial(exchange_kernel, n, g, s), out_shape=sha...]
    pallas_call x0 -> x1, Pallas kernels: none -> 157 us  [gather_weights(): pl.pallas_call(functools.partial(weight_kernel, n, len(small), tuple((axi...]
    psum x1 -> x0, blocking collectives: 43.8 us -> none  [local(): lax.psum(jnp.stack([grad_gain_attn, grad_gain_mlp]), ('rep', 'shard'))]
    dot_general x19 -> x15, matrix products: 40 us -> 38.9 us  [dot(): return jnp.dot(a, b, preferred_element_type=F32)]
    unnamed x124 -> x133, local copies, waits for them, and re-layouts: 16.7 us -> 17 us
where the time goes in v2:
time: 519 us; the launch traced here: 517 us
  Pallas kernels  411 us (79%)
  matrix products  47.2 us (9%)
  local copies, waits for them, and re-layouts  39.8 us (8%)
  other arithmetic  16.9 us (3%)
    pallas_call x1, Pallas kernels, gather_weights(): pl.pallas_call(functools.partial(weight_kernel, n, len(small), tuple((axi...  157 us
    pallas_call x1, Pallas kernels, rep_sum(): pl.pallas_call(functools.partial(rep_sum_kernel, zs, n), out_shape=[jax.S...  154 us
    pallas_call x3, Pallas kernels, exchange(): pl.pallas_call(functools.partial(exchange_kernel, n, g, s), out_shape=sha...  100 us
    dot_general x15, matrix products, dot(): return jnp.dot(a, b, preferred_element_type=F32)  38.9 us
    unnamed x133, local copies, waits for them, and re-layouts  17 us

profile of v2, /device:TPU:0, one launch (start us, length us, event | category | flops | bytes accessed | tf_op | source)
XLA Modules:
  0.0 516.8 jit_solution(18334883975094642241)
XLA Ops:
  2.9 3.4 concatenate.47.refs_2_
  6.4 1.9 copy.106.refs_5_
  9.5 156.9 %shard_map.212 = (s32[4,8,128]{2,1,0:T(8,128)}, bf16[4,16,240]{2,1,0:T(8,128)(2,1)}, bf16[4,240,2560]{2,1,0:T(8,128)(2,1)}, bf16[4,240,2560]{2,1,0:T(8,128)(2,1)...) custom-call(s32[8,128]{1,0:T(8,128)} %broadcast_in_dim.16.refs_0_, bf16[16,240]{1,0:T(8,128)(2,1)} %fusion.56.refs_1_, ...), custom_call_target="tpu_custom_call" | custom-call | tf_op jit(solution)/shard_map/pallas_call | solution.py:280
  168.1 3.3 fusion.6
  173.4 8.3 %shard_map.213 = bf16[4,128,640]{2,1,0:T(8,128)(2,1)} custom-call(bf16[128,640]{1,0:T(8,128)(2,1)} %pad_maximum_fusion.4.refs_0_), custom_call_target="tpu_custom_call" | custom-call | tf_op jit(solution)/shard_map/pallas_call | solution.py:129
  181.7 1.9 copy.109
  184.9 3.5 fusion.73
  188.4 2.6 fusion.16
  192.2 2.5 multiply_reduce_fusion.2
  195.0 3.4 fusion.75
  200.4 3.2 multiply_convert_fusion
  203.6 1.6 fusion.76
  205.3 2.2 multiply_reduce_fusion
  208.1 1.8 copy.113.refs_3_
  211.2 2.8 fusion.24
  218.2 1.4 copy.120
  219.6 2.4 fusion.28
  224.4 9.4 %shard_map.214 = bf16[4,128,640]{2,1,0:T(8,128)(2,1)} custom-call(bf16[4,128,640]{2,1,0:T(8,128)(2,1)} %pad_maximum_fusion.1.refs_0_), custom_call_target="tpu_custom_call" | custom-call | tf_op jit(solution)/shard_map/pallas_call | solution.py:129
  235.5 3.9 fusion.40
  246.1 82.3 %shard_map.215 = (bf16[4,128,2560]{2,1,0:T(8,128)(2,1)}, bf16[4,128,2560]{2,1,0:T(8,128)(2,1)}, bf16[4,128,2560]{2,1,0:T(8,128)(2,1)}, bf16[4,128,960]{2,1,0:T(8...) custom-call(bf16[128,2560]{1,0:T(8,128)(2,1)} %copy-done.11, ...), custom_call_target="tpu_custom_call" | custom-call | tf_op jit(solution)/shard_map/pallas_call | solution.py:129
  328.3 2.4 bitcast_convert_fusion
  330.7 1.9 copy.138
  332.7 2.2 convolution_convert_fusion.2
  334.9 2.3 convolution_convert_fusion.3
  338.1 2.8 convolution_convert_fusion
  341.0 1.9 convolution_convert_fusion.1
  344.3 154.4 %shard_map.216 = (f32[8,240]{1,0:T(8,128)S(1)}, bf16[2,4,32,2560]{3,2,1,0:T(8,128)(2,1)S(1)}, bf16[2,4,32,2560]{3,2,1,0:T(8,128)(2,1)S(1)}, bf16[2,4,32,2560]{3,...) custom-call(f32[8,240]{1,0:T(8,128)S(1)} %reduce_sum.99.refs_0_, bf16[2,4,32,2560]{3,2,1,0:T(8,128)(2,1)S(1)} %bitcast.147, ...), custom_call_target="tpu_custom_call" | custom-call | tf_op jit(solution)/shard_map/pallas_call | solution.py:397
  498.7 2.9 slice_convert_fusion
  501.6 1.9 bitcast_convert_fusion.1
  503.5 3.3 copy.143
  507.1 1.6 fusion.70
  512.6 3.3 fusion.23
  (203 shorter events, 35.3 us)
Async XLA Ops:
  0.6 5.7 %copy-start.18 = (bf16[640,960]{0,1:T(8,128)(2,1)S(1)}, bf16[640,960]{0,1:T(8,128)(2,1)}, u32[]{:S(2)}) copy-start(bf16[640,960]{0,1:T(8,128)(2,1)} %param.24) | copy-start | bytes 3686404
  2.9 5.4 %copy-start.52 = (bf16[240]{0:T(256)(128)(2,1)S(1)}, bf16[240]{0:T(256)(128)(2,1)}, u32[]{:S(2)}) copy-start(bf16[240]{0:T(256)(128)(2,1)} %param.16) | copy-start | bytes 1444
  2.9 5.4 %copy-start.53 = (bf16[240]{0:T(256)(128)(2,1)S(1)}, bf16[240]{0:T(256)(128)(2,1)}, u32[]{:S(2)}) copy-start(bf16[240]{0:T(256)(128)(2,1)} %param.21) | copy-start | bytes 1444
  2.9 6.0 %copy-start.49 = (s32[128]{0:T(128)S(1)}, s32[128]{0:T(128)}, u32[]{:S(2)}) copy-start(s32[128]{0:T(128)} %param.14) | copy-start | bytes 1540
  9.5 157.8 %copy-start.31 = (bf16[128,960]{0,1:T(8,128)(2,1)S(1)}, bf16[128,960]{0,1:T(8,128)(2,1)}, u32[]{:S(2)}) copy-start(bf16[128,960]{0,1:T(8,128)(2,1)} %param.13) | copy-start | bytes 737284
  167.7 4.6 copy-start.20
  183.8 4.5 copy-start.15
  184.0 4.4 copy-start.27
  184.0 4.4 copy-start.29
  194.9 3.7 slice-start.3
  195.0 5.1 slice-start.4
  198.7 6.6 %slice-start = ((s8[4915200]{0:T(1024)(128)(4,1)}), s8[4194304]{0:T(1024)(128)(4,1)S(1)}, s32[]{:S(2)}) async-start(s8[4915200]{0:T(1024)(128)(4,1)} %bitcast.152), calls=%async_computation | async-start | bytes 8388608
  200.4 4.9 slice-start.1
  207.5 6.5 %copy-start.3 = (f32[128,960]{1,0:T(8,128)}, f32[128,960]{1,0:T(8,128)S(1)}, u32[]{:S(2)}) copy-start(f32[128,960]{1,0:T(8,128)S(1)} %get-tuple-element.114) | copy-start | bytes 1474564
  209.9 4.2 copy-start.8
  209.9 4.3 copy-start.6
  209.9 4.3 copy-start.17
  209.9 4.3 copy-start.42
  223.3 12.2 %copy-start.24 = (bf16[128,15,64]{0,2,1:T(8,128)(2,1)S(1)}, bf16[128,15,64]{0,2,1:T(8,128)(2,1)}, u32[]{:S(2)}) copy-start(bf16[128,15,64]{0,2,1:T(8,128)(2,1)} %pad_maximum_fusion.3) | copy-start | bytes 737284
  223.3 12.2 %copy-start.38 = (f32[960]{0:T(1024)S(1)}, f32[960]{0:T(1024)}, u32[]{:S(2)}) copy-start(f32[960]{0:T(1024)} %copy-done.37) | copy-start | bytes 11524
  223.3 12.2 %copy-start.47 = (f32[128]{0:T(128)S(1)}, f32[128]{0:T(128)}, u32[]{:S(2)}) copy-start(f32[128]{0:T(128)} %copy-done.46) | copy-start | bytes 1540
  235.5 4.0 copy-start.40
  235.5 5.0 copy-start.23
  240.5 4.5 copy-start.21
  330.7 4.2 copy-start.50
  507.0 4.2 copy-start.4
  507.0 4.2 copy-start.5
  507.0 4.2 copy-start.26
  507.1 4.2 copy-start.36
  507.1 4.2 copy-start.45
  507.1 4.2 copy-start.48
  508.9 3.8 copy-start.13
  (29 other events, 62.7 us)

commit v3 on v2

--- a/solution.py
+++ b/solution.py
@@ -60,8 +60,8 @@
 
 def exchange_kernel(n, n_gather, n_scatter, *refs):
     total = n_gather + n_scatter
-    ins, outs = refs[:total], refs[total : 2 * total]
-    local_sem, send_sem, recv_sem = refs[2 * total :]
+    ins, outs, refs = refs[:total], refs[total : 2 * total], refs[2 * total :]
+    held, (local_sem, send_sem, recv_sem) = refs[:total], refs[total:]
     me = lax.axis_index("shard")
     chips = n // 2
     chip, core = me // 2, me % 2
@@ -105,9 +105,13 @@
     own = []
     for a in range(total):
         src = ins[a] if a < n_gather else ins[a].at[me]
-        copy = pltpu.make_async_copy(src, outs[a].at[me], local_sem.at[a])
+        copy = pltpu.make_async_copy(src, held[a], local_sem.at[a])
         copy.start()
         own.append(copy)
+    for a in range(total):
+        own[a].wait()
+        own[a] = pltpu.make_async_copy(held[a], outs[a].at[me], local_sem.at[total + a])
+        own[a].start()
     for a, k, copy in far:
         copy.wait_recv()
         origin = 2 * ((chip + chips - k) % chips) + core
@@ -131,12 +135,16 @@
         out_shape=shapes,
         in_specs=[pl.BlockSpec(memory_space=pl.ANY)] * (g + s),
         out_specs=[pl.BlockSpec(memory_space=pl.ANY)] * (g + s),
-        scratch_shapes=[
-            pltpu.SemaphoreType.DMA((g + s,)),
+        scratch_shapes=[pltpu.VMEM(a.shape, a.dtype) for a in gathers]
+        + [pltpu.VMEM(a.shape[1:], a.dtype) for a in scatters]
+        + [
+            pltpu.SemaphoreType.DMA((2 * (g + s),)),
             pltpu.SemaphoreType.DMA((copies,)),
             pltpu.SemaphoreType.DMA((copies,)),
         ],
-        compiler_params=pltpu.CompilerParams(collective_id=cid, has_side_effects=True),
+        compiler_params=pltpu.CompilerParams(
+            collective_id=cid, has_side_effects=True, vmem_limit_bytes=32 * 1024 * 1024
+        ),
     )(*gathers, *scatters)
     return out[:g], out[g:]
 
@@ -144,8 +152,8 @@
 def weight_kernel(n, n_small, axes, *refs):
     n_big = len(axes)
     total = n_small + n_big
-    ins, outs = refs[:total], refs[total : 2 * total]
-    local_sem, send_sem, recv_sem = refs[2 * total :]
+    ins, outs, refs = refs[:total], refs[total : 2 * total], refs[2 * total :]
+    held, (local_sem, send_sem, recv_sem) = refs[:total], refs[total:]
     me, rep = lax.axis_index("shard"), lax.axis_index("rep")
     chips = n // 2
     chip, core = me // 2, me % 2
@@ -206,31 +214,46 @@
             peer = {"shard": 2 * ((chip + k) % chips) + core}
             plain.append((a, k, remote(ins[a], outs[a].at[me], peer)))
         waits.append(remote(ins[a], outs[a].at[me], mate))
-    for a in range(n_small, total):
+
+    def start_direct(a):
         for k in range(1, chips):
             peer = {"shard": 2 * ((chip + k) % chips) + core}
             direct[a, k] = remote(
                 piece(ins[a], a, own_q), piece(outs[a].at[me], a, own_q), peer
             )
-    for a in range(n_small, total):
+
+    def start_corner(a):
         for k in range(1, chips):
             peer = {"shard": 2 * ((chip + k) % chips) + core}
             corner_x[a, k] = remote(
                 piece(ins[a], a, quarter_d, 0), piece(outs[a].at[me], a, quarter_d, 0), peer
             )
-        waits.append(remote(ins[a], outs[a].at[me], mate))
+
+    start_direct(n_small)
     own = []
     for a in range(total):
-        copy = pltpu.make_async_copy(ins[a], outs[a].at[me], local_sem.at[a])
+        if a >= n_small:
+            waits.append(remote(ins[a], outs[a].at[me], mate))
+        copy = pltpu.make_async_copy(ins[a], held[a], local_sem.at[a])
         copy.start()
         own.append(copy)
+    for a in range(total):
+        own[a].wait()
+        own[a] = pltpu.make_async_copy(held[a], outs[a].at[me], local_sem.at[total + a])
+        own[a].start()
 
     def origin(k):
         return 2 * ((chip + chips - k) % chips) + core
 
     def spread(a):
         for k in range(1, chips):
-            arrived(direct[a, k])
+            direct[a, k].wait()
+        if a + 1 < total:
+            start_direct(a + 1)
+        else:
+            for b in range(n_small, total):
+                start_corner(b)
+        for k in range(1, chips):
             block = piece(outs[a].at[origin(k)], a, own_q)
             side_a[a, k] = remote(block, block, near_a)
             side_b[a, k] = remote(block, block, near_b)
@@ -254,13 +277,13 @@
             arrived(corner_a[a, k])
             to_mate(piece(slot, a, quarter_d, 1))
 
-    for t in range(n_big + 2):
+    for t in range(n_big + 1):
         if t < n_big:
             spread(n_small + t)
         if 0 <= t - 1 < n_big:
             pass_on(n_small + t - 1)
-        if 0 <= t - 2 < n_big:
-            finish(n_small + t - 2)
+    for a in range(n_small, total):
+        finish(a)
     for a, k, copy in plain:
         arrived(copy)
         to_mate(outs[a].at[origin(k)])
@@ -282,12 +305,15 @@
         out_shape=[jax.ShapeDtypeStruct((n,) + a.shape, a.dtype) for a in arrays],
         in_specs=[pl.BlockSpec(memory_space=pl.ANY)] * total,
         out_specs=[pl.BlockSpec(memory_space=pl.ANY)] * total,
-        scratch_shapes=[
-            pltpu.SemaphoreType.DMA((total,)),
+        scratch_shapes=[pltpu.VMEM(a.shape, a.dtype) for a in arrays]
+        + [
+            pltpu.SemaphoreType.DMA((2 * total,)),
             pltpu.SemaphoreType.DMA((copies,)),
             pltpu.SemaphoreType.DMA((copies,)),
         ],
-        compiler_params=pltpu.CompilerParams(collective_id=cid, has_side_effects=True),
+        compiler_params=pltpu.CompilerParams(
+            collective_id=cid, has_side_effects=True, vmem_limit_bytes=32 * 1024 * 1024
+        ),
     )(*arrays)
 
 
@@ -325,7 +351,7 @@
         return copy
 
     gain_first = remote(gain_in, gain_near, partner)
-    first = [remote(ins[a].at[1 - side], near[a], partner) for a in range(n)]
+    first = [remote(ins[0].at[1 - side], near[0], partner)]
     second, third, fourth = {}, {}, {}
     gain_first.wait_recv()
     gain_pair[...] = gain_in[...] + gain_near[...]
@@ -336,7 +362,9 @@
     ]
 
     def pair_sum(a):
-        first[a].wait_recv()
+        first[a].wait()
+        if a + 1 < n:
+            first.append(remote(ins[a + 1].at[1 - side], near[a + 1], partner))
 
         def body(z, carry):
             sums[a][z] = (ins[a][side, z].astype(F32) + near[a][z].astype(F32)).astype(BF)
@@ -381,7 +409,6 @@
     gain_out[...] = value
     gain_first.wait_send()
     for a in range(n):
-        first[a].wait_send()
         for copy in second[a]:
             copy.wait_send()
         for copy in third[a]:

time: 519 us -> 421 us (0.81)
  Pallas kernels: 411 us -> 298 us
  local copies, waits for them, and re-layouts: 39.8 us -> 58.7 us
    pallas_call x1, Pallas kernels: 157 us -> 59.9 us  [gather_weights(): pl.pallas_call(functools.partial(weight_kernel, n, len(small), tuple((axi...]
    unnamed x133 -> x163, local copies, waits for them, and re-layouts: 17 us -> 33 us
    pallas_call x3, Pallas kernels: 100 us -> 84.4 us  [exchange(): pl.pallas_call(functools.partial(exchange_kernel, n, g, s), out_shape=sha...]
where the time goes in v3:
time: 421 us; the launch traced here: 418 us
  Pallas kernels  298 us (71%)
  local copies, waits for them, and re-layouts  58.7 us (14%)
  matrix products  45.2 us (11%)
  other arithmetic  14.2 us (3%)
    pallas_call x1, Pallas kernels, rep_sum(): pl.pallas_call(functools.partial(rep_sum_kernel, zs, n), out_shape=[jax.S...  153 us
    pallas_call x3, Pallas kernels, exchange(): pl.pallas_call(functools.partial(exchange_kernel, n, g, s), out_shape=sha...  84.4 us
    pallas_call x1, Pallas kernels, gather_weights(): pl.pallas_call(functools.partial(weight_kernel, n, len(small), tuple((axi...  59.9 us
    dot_general x15, matrix products, dot(): return jnp.dot(a, b, preferred_element_type=F32)  36.1 us
    unnamed x163, local copies, waits for them, and re-layouts  33 us

profile of v3, /device:TPU:0, one launch (start us, length us, event | category | flops | bytes accessed | tf_op | source)
XLA Modules:
  0.0 417.6 jit_solution(4166009975255759516)
XLA Ops:
  2.8 2.4 concatenate.47.refs_2_
  9.5 59.9 %shard_map.212 = (s32[4,8,128]{2,1,0:T(8,128)S(1)}, bf16[4,16,240]{2,1,0:T(8,128)(2,1)S(1)}, bf16[4,240,2560]{2,1,0:T(8,128)(2,1)S(1)}, bf16[4,240,2560]{2,1,0:T...) custom-call(s32[8,128]{1,0:T(8,128)S(1)} %broadcast_in_dim.16.refs_0_, ...), custom_call_target="tpu_custom_call" | custom-call | tf_op jit(solution)/shard_map/pallas_call | solution.py:303
  69.4 2.2 copy-done
  71.7 2.1 copy-done.1
  73.8 2.3 copy-done.13
  77.3 3.4 fusion.6
  82.0 7.7 %shard_map.213 = bf16[4,128,640]{2,1,0:T(8,128)(2,1)S(1)} custom-call(bf16[128,640]{1,0:T(8,128)(2,1)S(1)} %pad_maximum_fusion.4.refs_0_), custom_call_target="tpu_custom_call" | custom-call | tf_op jit(solution)/shard_map/pallas_call | solution.py:133
  91.3 3.4 fusion.73
  95.4 2.6 fusion.16
  98.4 2.8 multiply_reduce_fusion.2
  101.5 3.5 fusion.75
  107.1 3.2 multiply_convert_fusion
  112.0 2.2 multiply_reduce_fusion
  116.9 2.7 fusion.24
  123.7 1.8 concatenate.54
  125.4 1.9 copy.120
  127.4 2.4 fusion.28
  132.4 8.0 %shard_map.214 = bf16[4,128,640]{2,1,0:T(8,128)(2,1)S(1)} custom-call(bf16[4,128,640]{2,1,0:T(8,128)(2,1)S(1)} %pad_maximum_fusion.1.refs_0_), custom_call_target="tpu_custom_call" | custom-call | tf_op jit(solution)/shard_map/pallas_call | solution.py:133
  141.4 3.9 fusion.40
  145.7 1.6 copy.126
  152.5 1.8 copy.127
  154.3 1.8 copy.128
  157.1 68.7 %shard_map.215 = (bf16[4,128,2560]{2,1,0:T(8,128)(2,1)S(1)}, bf16[4,128,2560]{2,1,0:T(8,128)(2,1)S(1)}, bf16[4,128,2560]{2,1,0:T(8,128)(2,1)S(1)}, bf16[4,128,96...) custom-call(bf16[128,2560]{1,0:T(8,128)(2,1)S(1)} %get-tuple-element, ...), custom_call_target="tpu_custom_call" | custom-call | tf_op jit(solution)/shard_map/pallas_call | solution.py:133
  232.6 2.0 bitcast_convert_fusion
  234.6 2.5 copy.138
  240.0 2.8 convolution_convert_fusion
  242.7 1.9 convolution_convert_fusion.1
  246.0 153.4 %shard_map.216 = (f32[8,240]{1,0:T(8,128)S(1)}, bf16[2,4,32,2560]{3,2,1,0:T(8,128)(2,1)S(1)}, bf16[2,4,32,2560]{3,2,1,0:T(8,128)(2,1)S(1)}, bf16[2,4,32,2560]{3,...) custom-call(f32[8,240]{1,0:T(8,128)S(1)} %reduce_sum.99.refs_0_, bf16[2,4,32,2560]{3,2,1,0:T(8,128)(2,1)S(1)} %bitcast.155, ...), custom_call_target="tpu_custom_call" | custom-call | tf_op jit(solution)/shard_map/pallas_call | solution.py:424
  399.4 2.9 slice_convert_fusion
  402.3 2.0 bitcast_convert_fusion.1
  404.3 3.3 copy.143
  413.5 3.3 fusion.23
  (233 shorter events, 49.3 us)
Async XLA Ops:
  2.8 4.1 copy-start.68
  2.8 4.1 copy-start.65
  9.5 67.3 %copy-start.46 = (bf16[128,960]{0,1:T(8,128)(2,1)S(1)}, bf16[128,960]{0,1:T(8,128)(2,1)}, u32[]{:S(2)}) copy-start(bf16[128,960]{0,1:T(8,128)(2,1)} %param.13) | copy-start | bytes 737284
  77.0 21.4 %copy-start.26 = (bf16[128,960]{1,0:T(8,128)(2,1)}, bf16[128,960]{1,0:T(8,128)(2,1)S(1)}, u32[]{:S(2)}) copy-start(bf16[128,960]{1,0:T(8,128)(2,1)S(1)} %copy.103) | copy-start | bytes 737284
  77.3 4.3 %copy-start.35 = (bf16[128,960]{1,0:T(8,128)(2,1)}, bf16[128,960]{1,0:T(8,128)(2,1)S(1)}, u32[]{:S(2)}) copy-start(bf16[128,960]{1,0:T(8,128)(2,1)S(1)} %fusion.32) | copy-start | bytes 737284
  82.0 9.2 %copy-start.66 = (s32[128]{0:T(128)S(1)}, s32[128]{0:T(128)}, u32[]{:S(2)}) copy-start(s32[128]{0:T(128)} %param.14) | copy-start | bytes 1540
  98.4 21.3 %copy-start.32 = (bf16[5,64,128,3]{2,1,3,0:T(8,128)(2,1)}, bf16[5,64,128,3]{2,1,3,0:T(8,128)(2,1)S(1)}, u32[]{:S(2)}) copy-start(bf16[5,64,128,3]{2,1,3,0:T(8,128)(2,1)S(1)} %convolution_convert_fusion.4) | copy-start | bytes 737284
  101.2 14.6 %copy-start.20 = (f32[128,960]{1,0:T(8,128)}, f32[128,960]{1,0:T(8,128)S(1)}, u32[]{:S(2)}) copy-start(f32[128,960]{1,0:T(8,128)S(1)} %get-tuple-element.113) | copy-start | bytes 1474564
  101.3 10.7 %copy-start.59 = (f32[128]{0:T(128)}, f32[128]{0:T(128)S(1)}, u32[]{:S(2)}) copy-start(f32[128]{0:T(128)S(1)} %add_rsqrt_fusion) | copy-start | bytes 1540
  101.4 14.5 %copy-start.50 = (f32[960]{0:T(1024)}, f32[960]{0:T(1024)S(1)}, u32[]{:S(2)}) copy-start(f32[960]{0:T(1024)S(1)} %reshape.328) | copy-start | bytes 11524
  101.5 5.2 %slice-start.4 = ((s8[5242880]{0:T(1024)(128)(4,1)}), s8[4194304]{0:T(1024)(128)(4,1)S(1)}, s32[]{:S(2)}) async-start(s8[5242880]{0:T(1024)(128)(4,1)} %bitcast.177), calls=%async_computation.4 | async-start | bytes 8388608
  105.4 6.5 %slice-start = ((s8[4915200]{0:T(1024)(128)(4,1)}), s8[4194304]{0:T(1024)(128)(4,1)S(1)}, s32[]{:S(2)}) async-start(s8[4915200]{0:T(1024)(128)(4,1)} %bitcast.146), calls=%async_computation | async-start | bytes 8388608
  107.1 4.8 %slice-start.1 = ((s8[4915200]{0:T(1024)(128)(4,1)}), s8[720896]{0:T(1024)(128)(4,1)S(1)}, s32[]{:S(2)}) async-start(s8[4915200]{0:T(1024)(128)(4,1)} %bitcast.146), calls=%async_computation.1 | async-start | bytes 1441792
  114.2 5.5 %copy-start.29 = (f32[128,960]{1,0:T(8,128)}, f32[128,960]{1,0:T(8,128)S(1)}, u32[]{:S(2)}) copy-start(f32[128,960]{1,0:T(8,128)S(1)} %get-tuple-element.114) | copy-start | bytes 1474564
  121.4 6.0 %copy-start.23 = (bf16[128,5,3,512]{0,3,2,1:T(8,128)(2,1)S(1)}, bf16[128,5,3,512]{0,3,2,1:T(8,128)(2,1)}, u32[]{:S(2)}) copy-start(bf16[128,5,3,512]{0,3,2,1:T(8,128)(2,1)} %copy-done.22) | copy-start | bytes 5898244
  130.8 9.8 %copy-start.49 = (f32[128,32]{0,1:T(8,128)S(1)}, f32[128,32]{0,1:T(8,128)}, u32[]{:S(2)}) copy-start(f32[128,32]{0,1:T(8,128)} %get-tuple-element.107) | copy-start | bytes 49156
  131.1 10.3 %copy-start.27 = (bf16[128,960]{1,0:T(8,128)(2,1)S(1)}, bf16[128,960]{1,0:T(8,128)(2,1)}, u32[]{:S(2)}) copy-start(bf16[128,960]{1,0:T(8,128)(2,1)} %copy-done.26) | copy-start | bytes 737284
  131.1 10.2 %copy-start.37 = (bf16[128,15,64]{0,2,1:T(8,128)(2,1)S(1)}, bf16[128,15,64]{0,2,1:T(8,128)(2,1)}, u32[]{:S(2)}) copy-start(bf16[128,15,64]{0,2,1:T(8,128)(2,1)} %pad_maximum_fusion.3) | copy-start | bytes 737284
  131.1 10.2 %copy-start.53 = (f32[960]{0:T(1024)S(1)}, f32[960]{0:T(1024)}, u32[]{:S(2)}) copy-start(f32[960]{0:T(1024)} %copy-done.52) | copy-start | bytes 11524
  131.1 10.2 %copy-start.62 = (f32[128]{0:T(128)S(1)}, f32[128]{0:T(128)}, u32[]{:S(2)}) copy-start(f32[128]{0:T(128)} %copy-done.61) | copy-start | bytes 1540
  141.4 4.1 copy-start.38
  145.3 5.8 %copy-start.25 = (bf16[128,960]{1,0:T(8,128)(2,1)S(1)}, bf16[128,960]{1,0:T(8,128)(2,1)}, u32[]{:S(2)}) copy-start(bf16[128,960]{1,0:T(8,128)(2,1)} %copy-done.24) | copy-start | bytes 737284
  232.6 4.5 %copy-start.15 = (bf16[4,128,2560]{2,1,0:T(8,128)(2,1)S(1)}, bf16[4,128,2560]{2,1,0:T(8,128)(2,1)}, u32[]{:S(2)}) copy-start(bf16[4,128,2560]{2,1,0:T(8,128)(2,1)} %copy-done.14) | copy-start | bytes 7864324
  407.8 4.2 %copy-start.21 = (f32[128,960]{1,0:T(8,128)S(1)}, f32[128,960]{1,0:T(8,128)}, u32[]{:S(2)}) copy-start(f32[128,960]{1,0:T(8,128)} %copy-done.20) | copy-start | bytes 1474564
  407.8 4.2 %copy-start.28 = (bf16[128,960]{1,0:T(8,128)(2,1)S(1)}, bf16[128,960]{1,0:T(8,128)(2,1)}, u32[]{:S(2)}) copy-start(bf16[128,960]{1,0:T(8,128)(2,1)} %copy-done.26) | copy-start | bytes 737284
  407.8 4.2 %copy-start.30 = (f32[128,960]{1,0:T(8,128)S(1)}, f32[128,960]{1,0:T(8,128)}, u32[]{:S(2)}) copy-start(f32[128,960]{1,0:T(8,128)} %copy-done.29) | copy-start | bytes 1474564
  407.8 4.2 %copy-start.40 = (f32[128,960]{1,0:T(8,128)S(1)}, f32[128,960]{1,0:T(8,128)}, u32[]{:S(2)}) copy-start(f32[128,960]{1,0:T(8,128)} %get-tuple-element.115) | copy-start | bytes 1474564
  407.8 4.2 %copy-start.51 = (f32[960]{0:T(1024)S(1)}, f32[960]{0:T(1024)}, u32[]{:S(2)}) copy-start(f32[960]{0:T(1024)} %copy-done.50) | copy-start | bytes 11524
  407.9 4.2 %copy-start.54 = (f32[960]{0:T(1024)S(1)}, f32[960]{0:T(1024)}, u32[]{:S(2)}) copy-start(f32[960]{0:T(1024)} %copy-done.52) | copy-start | bytes 11524
  407.9 4.2 %copy-start.60 = (f32[128]{0:T(128)S(1)}, f32[128]{0:T(128)}, u32[]{:S(2)}) copy-start(f32[128]{0:T(128)} %copy-done.59) | copy-start | bytes 1540
  407.9 4.2 %copy-start.63 = (f32[128]{0:T(128)S(1)}, f32[128]{0:T(128)}, u32[]{:S(2)}) copy-start(f32[128]{0:T(128)} %copy-done.61) | copy-start | bytes 1540
  407.9 4.2 %copy-start.64 = (f32[128]{0:T(128)S(1)}, f32[128]{0:T(128)}, u32[]{:S(2)}) copy-start(f32[128]{0:T(128)} %broadcast_multiply_fusion.2) | copy-start | bytes 1540
  (44 other events, 105.8 us)
